TPU v7x, 256 devices: a whole 4x4x8 slice. The times are simulated.
256 devices in a mesh: ctx: 32 (over x, y, core), ch: 8 (over z).
Axes of the slice: x: 4, y: 4, z: 8, core: 2. Of those that a mesh axis runs over, the one named last changes fastest.
Arguments:
- projected: bfloat16 [3, 6144, 4096], P(None, 'ctx', 'ch'), may hold values from -6 to 6
- short_filter: float32 [7, 3, 4096], P(None, None, 'ch'), may hold values from -2.5 to 2.5
- medium_filter: bfloat16 [128, 4096], P(None, 'ch'), may hold values from -1.25 to 1.25
- decay: float32 [16, 4096], P(None, 'ch'), may hold values from 3.2552085e-05 to 0.05
- residues: float32 [16, 4096], P(None, 'ch'), may hold values from -3 to 3
- skip_gain: float32 [4096], P('ch'), may hold values from -6 to 6
- out_gain: float32 [4096], P('ch'), may hold values from 0.25 to 1.75
Outputs:
- mixed: bfloat16 [6144, 4096], P('ctx', 'ch')
All inputs are finite; a program needn't handle non-finite values.
Results may differ from a plain program's by a relative error of at most 0.014.
Values may be sent and summed in bfloat16 or wider, within the bound.
No kernel may reach another device: no remote copies, remote signals or barrier semaphores. Data moves between devices by JAX's collectives and lax.ppermute only.
A program may use at most 64 MiB of HBM per device.

v0:
```python
import jax
import jax.numpy as jnp
from jax import lax
from jax.sharding import PartitionSpec as P

C = 4096
SHORT = 7
MED = 128


norm_eps = 1e-06
block_len = 32


def from_behind(block, axis, distance):
    devices = range(lax.axis_size(axis))
    route = [(i - distance, i) for i in devices if i - distance in devices]
    return lax.ppermute(block, axis, route)


def causal_taps(extended, tap_weights, out_rows):
    running = tap_weights[SHORT - 1][None, :] * extended[:out_rows].astype(jnp.float32)
    for delay_step in range(SHORT - 1):
        offset_row = SHORT - 1 - delay_step
        running = running + tap_weights[delay_step][None, :] * extended[
            offset_row : offset_row + out_rows
        ].astype(jnp.float32)
    return running


def delay_selector(row_total, col_total, shift_base, tap_total, dtype):
    out_row = jnp.arange(row_total)[:, None, None]
    in_row = jnp.arange(col_total)[None, :, None]
    tap_row = jnp.arange(tap_total)[None, None, :]
    picked = tap_row == shift_base + out_row - in_row
    return picked.astype(dtype).reshape(row_total * col_total, tap_total)


def split_parts(table):
    upper = table.astype(jnp.bfloat16)
    lower = (table - upper.astype(jnp.float32)).astype(jnp.bfloat16)
    return (upper, lower)


def wide_einsum(form, left, right):
    return jnp.einsum(form, left, right, preferred_element_type=jnp.float32)


def medium_conv(extended, medium_filter):
    chan_count = extended.shape[1]
    row_count = extended.shape[0] - (MED - 1)
    block_total = row_count // block_len
    padded = jnp.concatenate([jnp.zeros((1, chan_count), extended.dtype), extended], 0)
    windows = jnp.concatenate(
        [
            padded[part_index * block_len : part_index * block_len + row_count].reshape(
                block_total, block_len, chan_count
            )
            for part_index in range(MED // block_len + 1)
        ],
        1,
    )
    span_width = MED + block_len
    selector = delay_selector(block_len, span_width, MED, MED, jnp.bfloat16)
    band_table = (
        jnp.dot(selector, medium_filter, preferred_element_type=jnp.float32)
        .astype(jnp.bfloat16)
        .reshape(block_len, span_width, chan_count)
    )
    mixed_rows = jnp.einsum("bsc,tsc->btc", windows, band_table, preferred_element_type=jnp.float32)
    return mixed_rows.reshape(row_count, chan_count).astype(jnp.bfloat16)


def compose(earlier, later):
    return (earlier[0] * later[0], later[0] * earlier[1] + later[1])


def on_device(projected, short_filter, medium_filter, decay, residues, skip_gain, out_gain):
    row_count = projected.shape[1]
    chan_count = projected.shape[2]
    short_lead = SHORT - 1
    med_reach = MED - 1
    prior_rows = from_behind(projected[:, row_count - short_lead :], "ctx", 1)
    full_ext = jnp.concatenate([prior_rows, projected], 1)
    queries = causal_taps(full_ext[0], short_filter[:, 0], row_count)
    key_feats = causal_taps(full_ext[1], short_filter[:, 1], row_count)
    values = causal_taps(full_ext[2], short_filter[:, 2], row_count)
    rounded = lax.optimization_barrier(jnp.stack([key_feats, values]).astype(jnp.bfloat16)).astype(
        jnp.float32
    )
    own_product = (rounded[0] * rounded[1]).astype(jnp.bfloat16)
    prior_product = from_behind(own_product[row_count - med_reach :], "ctx", 1)
    extended = jnp.concatenate([prior_product, own_product], 0)
    queries = lax.optimization_barrier(queries.astype(jnp.bfloat16)).astype(jnp.float32)
    mediated = lax.optimization_barrier(medium_conv(extended, medium_filter))
    med_float = mediated.astype(jnp.float32)
    weights = residues * jnp.sqrt(-jnp.expm1(-2.0 * decay))
    block_total = row_count // block_len
    steps_in = jnp.arange(block_len).astype(jnp.float32)
    decay_table = jnp.exp(-decay[:, None, :] * steps_in[None, :, None])
    head_kernel = jnp.sum(weights[:, None, :] * decay_table, 0)
    head_selector = delay_selector(block_len, block_len, 0, block_len, jnp.float32)
    band_table = jnp.dot(
        head_selector,
        head_kernel,
        precision=lax.Precision.HIGHEST,
        preferred_element_type=jnp.float32,
    ).reshape(block_len, block_len, chan_count)
    blocks = mediated.reshape(block_total, block_len, chan_count)
    band_upper, band_lower = split_parts(band_table)
    within = wide_einsum("bsc,tsc->btc", blocks, band_upper) + wide_einsum(
        "bsc,tsc->btc", blocks, band_lower
    )
    reach_upper, reach_lower = split_parts(decay_table[:, ::-1])
    summaries = wide_einsum("bsc,nsc->bnc", blocks, reach_upper) + wide_einsum(
        "bsc,nsc->bnc", blocks, reach_lower
    )
    step_decay = jnp.exp(-decay * block_len)
    _, inclusive = lax.associative_scan(
        compose, (jnp.broadcast_to(step_decay[None], summaries.shape), summaries), axis=0
    )
    local_end = inclusive[-1]
    local_start = jnp.concatenate([jnp.zeros_like(inclusive[:1]), inclusive[:-1]], 0)
    own_index = lax.axis_index("ctx")
    span_rates = decay * row_count
    shard_part = lax.all_gather(
        local_end[None].astype(jnp.bfloat16), "ctx", axis=0, tiled=True
    ).astype(jnp.float32)
    distance = own_index - 1 - jnp.arange(shard_part.shape[0])
    factor = jnp.where(
        (distance >= 0)[:, None, None],
        jnp.exp(-span_rates[None] * jnp.maximum(distance, 0).astype(jnp.float32)[:, None, None]),
        0.0,
    )
    carried = jnp.zeros_like(local_end) + jnp.sum(factor * shard_part, 0)
    block_index = jnp.arange(block_total).astype(jnp.float32)
    entry_states = (
        local_start
        + jnp.exp(-decay[None] * (block_len * block_index)[:, None, None]) * carried[None]
    )
    out_table = weights[:, None, :] * jnp.exp(-decay[:, None, :] * (steps_in[None, :, None] + 1.0))
    state_upper, state_lower = split_parts(entry_states)
    table_upper, table_lower = split_parts(out_table)
    from_prior = (
        wide_einsum("bnc,ntc->btc", state_upper, table_upper)
        + wide_einsum("bnc,ntc->btc", state_upper, table_lower)
        + wide_einsum("bnc,ntc->btc", state_lower, table_upper)
    )
    summed = (within + from_prior).reshape(row_count, chan_count) + skip_gain[None, :] * med_float
    gated_out = queries * summed
    square_sum = lax.psum(jnp.sum(gated_out * gated_out, axis=1), "ch")
    inv_rms = lax.rsqrt(square_sum / C + norm_eps)
    return (gated_out * inv_rms[:, None] * out_gain[None, :]).astype(jnp.bfloat16)


def solution(mesh):
    in_specs = (
        P(None, "ctx", "ch"),
        P(None, None, "ch"),
        P(None, "ch"),
        P(None, "ch"),
        P(None, "ch"),
        P("ch"),
        P("ch"),
    )
    out_specs = P("ctx", "ch")
    return jax.shard_map(
        on_device, mesh=mesh, in_specs=in_specs, out_specs=out_specs, check_vma=False
    )
```

profile of v0, /device:TPU:1, one launch (start us, length us, event | category | flops | bytes accessed | tf_op | source)
XLA Modules:
  0.0 696.1 jit_solution(13937085966700101513)
XLA Ops:
  0.8 4.6 collective-permute-start
  9.1 1.4 multiply_negate_fusion
  10.8 4.0 convolution_convert_fusion
  14.8 6.9 multiply_reduce_fusion
  22.8 14.0 %copy.84 = bf16[32,160,512]{1,0,2:T(8,128)(2,1)} copy(bf16[32,160,512]{2,1,0:T(8,128)(2,1)} %bitcast.92) | data formatting | bytes 10485760 | tf_op jit(solution)/shard_map/reshape | solution.py:68
  36.8 7.2 %rev.3 = f32[16,32,512]{1,0,2:T(8,128)} reverse(f32[16,32,512]{1,0,2:T(8,128)} %get-tuple-element.15), dimensions={1} | reverse | bytes 2097152 | tf_op jit(solution)/shard_map/rev | solution.py:114
  44.0 6.4 copy.87
  50.5 6.5 copy.89
  57.9 2.1 collective-permute-start.1
  62.0 1.9 copy.85
  63.9 5.6 fusion.17
  71.0 3.5 fusion.23
  74.5 1.2 add_bitcast_fusion.1
  75.8 6.7 slice.347
  82.5 6.6 slice.346
  89.0 6.4 slice.353
  95.4 1.9 multiply_add_fusion.1
  98.7 6.8 pad.14
  106.0 154.0 %pad.17 = f32[6,16,512]{1,0,2:T(8,128)} pad(f32[3,16,512]{1,0,2:T(4,128)S(1)} %pad_add_fusion, f32[]{:T(128)} %constant.14.clone.1), padding=1_0_1x0_0_0x0_0_0 | pad | bytes 294916 | tf_op jit(solution)/shard_map/pad | solution.py:119
  259.9 153.8 %pad.205 = f32[5,16,512]{1,0,2:T(8,128)} pad(f32[3,16,512]{1,0,2:T(4,128)S(1)} %pad_add_fusion, f32[]{:T(128)} %constant.14.clone.1), padding=0_0_1x0_0_0x0_0_0 | pad | bytes 262148
  413.7 1.8 fusion.27
  415.6 1.5 pad_maximum_fusion
  417.1 216.8 %pad.16 = f32[6,16,512]{1,0,2:T(8,128)} pad(f32[3,16,512]{1,0,2:T(4,128)} %pad_maximum_fusion, f32[]{:T(128)} %constant.14.clone.1), padding=0_1_1x0_0_0x0_0_0 | pad | bytes 294916 | tf_op jit(solution)/shard_map/pad | solution.py:119
  633.9 1.9 add_convert_fusion.2
  635.9 27.9 %all_gather.3 = bf16[32,16,512]{2,1,0:T(8,128)(2,1)S(1)} all-gather(bf16[1,16,512]{2,1,0:T(8,128)(2,1)S(1)} %copy.93), channel_id=1, replica_groups=mesh['ctx'=32,'ch'=8] {'ctx'}, dimensions={0}, use_global_device_ids=true | all-gather | bytes 540672 | tf_op jit(solution)/shard_map/all_gather | solution.py:126
  664.2 1.9 slice_add_fusion
  666.2 2.3 fusion.1
  668.5 2.3 fusion.3
  670.9 2.3 fusion.5
  673.3 2.2 fusion.73
  675.5 2.3 add_bitcast_fusion
  679.0 16.3 %psum.7 = f32[192]{0:T(256)S(1)} all-reduce(f32[192]{0:T(256)S(1)} %multiply_reduce_fusion.2), channel_id=1, replica_groups=mesh['ctx'=32,'ch'=8] {'ch'}, use_global_device_ids=true, to_apply=%region_3.4 | all-reduce | flops 192 | bytes 1536 | tf_op jit(solution)/shard_map/psum | solution.py:151
  (91 shorter events, 14.3 us)
Async XLA Ops:
  0.0 10.8 %copy-start = (bf16[128,512]{1,0:T(8,128)(2,1)S(1)}, bf16[128,512]{1,0:T(8,128)(2,1)}, u32[]{:S(2)}) copy-start(bf16[128,512]{1,0:T(8,128)(2,1)} %param.9) | copy-start | bytes 393220
  0.8 56.2 %collective-permute-start = (bf16[3,6,512]{2,1,0:T(8,128)(2,1)S(1)}, bf16[3,6,512]{2,1,0:T(8,128)(2,1)S(1)}, u32[]{:S(2)}, u32[]{:S(2)}) collective-permute-start(bf16[3,6,512]{2,1,0:T(8,128)(2,1)S(1)} %slice.293), channel_id=1, source_target_pairs={{0,8},{8,16},{16,24},{24,32},{32,40},{40,48},{48,56},{56,64},{64,7... | collective-permute-start | bytes 55304 | tf_op jit(solution)/shard_map/ppermute | solution.py:18
  9.1 5.7 copy-start.14
  9.1 86.3 %copy-start.9 = (f32[16,512]{0,1:T(8,128)}, f32[16,512]{0,1:T(8,128)S(1)}, u32[]{:S(2)}) copy-start(f32[16,512]{0,1:T(8,128)S(1)} %get-tuple-element.17) | copy-start | bytes 98308
  10.6 4.2 copy-start.12
  50.5 6.5 copy-start.6
  57.9 3.9 collective-permute-start.1
  70.2 0.8 copy-start.10
  71.0 3.5 copy-start.2
  75.7 19.7 %copy-start.5 = (f32[6,16,512]{1,0,2:T(8,128)}, f32[6,16,512]{1,0,2:T(8,128)S(1)}, u32[]{:S(2)}) copy-start(f32[6,16,512]{1,0,2:T(8,128)S(1)} %add_bitcast_fusion.1) | copy-start | bytes 589828
  95.4 2.0 copy-start.16
  98.1 7.9 %copy-start.8 = (f32[1,16,512]{1,0,2:T(1,128)}, f32[1,16,512]{1,0,2:T(1,128)S(1)}, u32[]{:S(2)}) copy-start(f32[1,16,512]{1,0,2:T(1,128)S(1)} %get-tuple-element.8) | copy-start | bytes 98308
  259.9 155.6 %slice-start = ((f32[6,16,512]{1,0,2:T(8,128)}), f32[1,16,512]{1,0,2:T(1,128)S(1)}, s32[]{:S(2)}) async-start(f32[6,16,512]{1,0,2:T(8,128)} %copy-done.5), calls=%async_computation | async-start | bytes 524288 | tf_op jit(solution)/shard_map/slice | solution.py:119
  417.1 246.6 %copy-start.18 = (f32[16,512]{1,0:T(8,128)S(1)}, f32[16,512]{1,0:T(8,128)}, u32[]{:S(2)}) copy-start(f32[16,512]{1,0:T(8,128)} %get-tuple-element.40) | copy-start | bytes 98308
  417.1 247.1 %copy-start.7 = (f32[6,16,512]{1,0,2:T(8,128)S(1)}, f32[6,16,512]{1,0,2:T(8,128)}, u32[]{:S(2)}) copy-start(f32[6,16,512]{1,0,2:T(8,128)} %pad.17) | copy-start | bytes 589828
  664.2 1.9 copy-start.13
  664.2 1.9 copy-start.15
  670.9 2.4 copy-start.3
  673.2 2.3 copy-start.4
  675.5 20.6 %copy-start.1 = (bf16[128,512]{1,0:T(8,128)(2,1)S(1)}, bf16[128,512]{1,0:T(8,128)(2,1)}, u32[]{:S(2)}) copy-start(bf16[128,512]{1,0:T(8,128)(2,1)} %param.9) | copy-start | bytes 393220
  677.8 0.9 copy-start.11
  677.8 1.0 copy-start.17
  677.8 1.0 copy-start.19
  677.8 17.5 %copy-start.20 = (f32[512]{0:T(512)S(1)}, f32[512]{0:T(512)}, u32[]{:S(2)}) copy-start(f32[512]{0:T(512)} %param.13) | copy-start | bytes 6148
where the time goes:
time: 708 us; the launch traced here: 696 us
  local copies, waits for them, and re-layouts  594 us (84%)
  blocking collectives  44.1 us (6%)
  matrix products  27 us (4%)
  other arithmetic  23.4 us (3%)
    pad x3, local copies, waits for them, and re-layouts, on_device(): lax.associative_scan(compose, (jnp.broadcast_to(step_decay[None], summari...  378 us
    unnamed x48, local copies, waits for them, and re-layouts  155 us
    all_gather x1, blocking collectives, on_device(): lax.all_gather(local_end[None].astype(jnp.bfloat16), 'ctx', axis=0, tiled...  27.9 us
    slice x5, local copies, waits for them, and re-layouts, on_device(): lax.associative_scan(compose, (jnp.broadcast_to(step_decay[None], summari...  19.7 us
    dot_general x7, matrix products, wide_einsum(): return jnp.einsum(form, left, right, preferred_element_type=jnp.float32)  16.3 us
    psum x1, blocking collectives, on_device(): square_sum = lax.psum(jnp.sum(gated_out * gated_out, axis=1), 'ch')  16.3 us
  transfers between devices with their start and end apart: 2, of which 1 were waited for; matrix products, arithmetic and copies ran while one was open for 8% of the time, Pallas kernels for 0%

commit v1 on v0

v1 whole, which is shorter than its diff:
```python
import functools
import jax
import jax.numpy as jnp
from jax import lax
from jax.experimental import pallas as pl
from jax.experimental.pallas import tpu as pltpu
from jax.sharding import PartitionSpec as P

C = 4096
SHORT = 7
MED = 128
MODES = 16
EPS = 1e-06
LANES = 128
TILE = 8
F32 = jnp.float32
BF16 = jnp.bfloat16
PARAMS = pltpu.CompilerParams(vmem_limit_bytes=48 * 1024 * 1024)


def row_iota():
    return lax.broadcasted_iota(jnp.int32, (TILE, LANES), 0).astype(F32)


def lanes_of(group):
    return pl.ds(pl.multiple_of(group * LANES, LANES), LANES)


def one_minus_exp(x):
    return x * (1 - x * (1 / 2) * (1 - x * (1 / 3) * (1 - x * (1 / 4) * (1 - x * (1 / 5) * (1 - x * (1 / 6))))))


def tiles_of(array):
    return [array[TILE * i : TILE * (i + 1)] for i in range(array.shape[0] // TILE)]


def filter_kernel(med_ref, decay_ref, res_ref, skip_ref, g_ref, wm_ref, med_f32, shifted):
    med_tiles = MED // TILE
    far_tiles = g_ref.shape[0] // TILE - med_tiles

    def group_body(group, _):
        cols = lanes_of(group)
        rows = row_iota()
        decay = decay_ref[:, cols]
        weights = res_ref[:, cols] * jnp.sqrt(one_minus_exp(2.0 * decay))
        eight = jnp.exp(-TILE * decay)
        med = med_ref[:, cols].astype(F32)
        med_f32[...] = med
        near = [jnp.zeros((TILE, LANES), F32) for _ in range(med_tiles)]
        far = [jnp.zeros((TILE, LANES), F32) for _ in range(far_tiles)]
        for n in range(MODES):
            rate = decay[n : n + 1]
            step = jnp.broadcast_to(eight[n : n + 1], (TILE, LANES))
            weight = weights[n : n + 1]
            powers = jnp.exp(-rate * rows)
            term = weight * powers
            state = jnp.zeros((TILE, LANES), F32)
            for i in range(med_tiles):
                near[i] = near[i] + term
                term = term * step
                state = state * step + med[TILE * i : TILE * (i + 1)]
            reach = jnp.sum(state * jnp.exp(-rate * (TILE - 1 - rows)), axis=0, keepdims=True)
            reach = reach * weight
            wm_ref[n : n + 1, cols] = reach
            term = reach * jnp.exp(-rate * (rows + 1))
            for i in range(far_tiles):
                far[i] = far[i] + term
                term = term * step
        near[0] = near[0] + jnp.where(rows == 0, skip_ref[:, cols], 0.0)
        taps = jnp.concatenate(near, 0)
        for s in range(TILE):
            shifted[s, 0:TILE] = jnp.zeros((TILE, LANES), F32)
            shifted[s, s : s + MED] = taps

        def shift_body(s, acc):
            acc = list(acc)
            bank = [shifted[s, TILE * i : TILE * (i + 1)] for i in range(med_tiles)]
            for j in range(med_tiles):
                row = jnp.broadcast_to(med_f32[pl.ds(TILE * j + s, 1), :], (TILE, LANES))
                for i in range(j, med_tiles):
                    acc[i] = acc[i] + row * bank[i - j]
            return tuple(acc)

        acc = lax.fori_loop(0, TILE, shift_body, tuple(jnp.zeros((TILE, LANES), F32) for _ in range(med_tiles)))
        g_ref[:, cols] = jnp.concatenate(list(acc) + far, 0)
        return 0

    lax.fori_loop(0, g_ref.shape[1] // LANES, group_body, 0)


def feature_kernel(proj_ref, halo_ref, short_ref, decay_ref, q_ref, p_ref, tail_ref, spread_ref, ext):
    row_count = proj_ref.shape[1]
    all_tiles = row_count // TILE
    part_tiles = all_tiles - MED // TILE

    def group_body(group, _):
        cols = lanes_of(group)
        rows = row_iota()
        feats = []
        for j in range(3):
            ext[j, 0:TILE] = halo_ref[j, :, cols].astype(F32)[TILE : 2 * TILE]
            ext[j, TILE : TILE + row_count] = proj_ref[j, :, cols].astype(F32)
            total = short_ref[0, j : j + 1, cols] * ext[j, TILE : TILE + row_count]
            for d in range(1, SHORT):
                total = total + short_ref[d, j : j + 1, cols] * ext[j, TILE - d : TILE - d + row_count]
            feats.append(total.astype(BF16))
        q_ref[:, cols] = feats[0]
        product = (feats[1].astype(F32) * feats[2].astype(F32)).astype(BF16)
        p_ref[:, cols] = product
        tail_ref[0:MED, cols] = product[row_count - MED :]
        tiles = tiles_of(product.astype(F32))
        decay = decay_ref[:, cols]
        eight = jnp.exp(-TILE * decay)
        parts, wholes = [], []
        for n in range(MODES):
            step = jnp.broadcast_to(eight[n : n + 1], (TILE, LANES))
            close = jnp.exp(-decay[n : n + 1] * (TILE - 1 - rows))
            state = tiles[0]
            for i in range(1, all_tiles):
                if i == part_tiles:
                    parts.append(jnp.sum(state * close, axis=0, keepdims=True))
                state = state * step + tiles[i]
            wholes.append(jnp.sum(state * close, axis=0, keepdims=True))
        tail_ref[MED : MED + MODES, cols] = jnp.concatenate(parts, 0).astype(BF16)
        whole = jnp.concatenate(wholes, 0).astype(BF16)
        for i in range(spread_ref.shape[0]):
            spread_ref[i, :, cols] = whole
        return 0

    lax.fori_loop(0, q_ref.shape[1] // LANES, group_body, 0)


def mix_kernel(index_ref, g_ref, wm_ref, decay_ref, states_ref, tail_ref, p_ref, q_ref, gated_ref, sums_ref,
               shifted, signal, squares):
    row_count = p_ref.shape[0]
    out_tiles = row_count // TILE
    lead_tiles = MED // TILE
    reach = g_ref.shape[0]
    own = index_ref[0]
    squares[...] = jnp.zeros(squares.shape, F32)

    def group_body(group, _):
        cols = lanes_of(group)
        rows = row_iota()
        for s in range(TILE):
            shifted[s, 0:TILE] = jnp.zeros((TILE, LANES), F32)
            shifted[s, s : s + reach] = g_ref[:, cols]
        tail = tail_ref[:, cols].astype(F32)
        signal[0:MED] = tail[0:MED]
        signal[MED : MED + row_count] = p_ref[:, cols].astype(F32)
        decay = decay_ref[:, cols]
        span = jnp.exp(-float(row_count) * decay)

        def carry_body(j, carried):
            return carried * span + states_ref[j, :, cols].astype(F32)

        carried = lax.fori_loop(0, own - 1, carry_body, jnp.zeros((MODES, LANES), F32))
        carried = tail[MED : MED + MODES] + jnp.exp(-float(row_count - MED) * decay) * carried
        carried = carried * wm_ref[:, cols]
        eight = jnp.exp(-TILE * decay)
        acc = [jnp.zeros((TILE, LANES), F32) for _ in range(out_tiles)]
        for n in range(MODES):
            step = jnp.broadcast_to(eight[n : n + 1], (TILE, LANES))
            term = carried[n : n + 1] * jnp.exp(-decay[n : n + 1] * (rows + 2))
            for i in range(out_tiles):
                acc[i] = acc[i] + term
                term = term * step

        def shift_body(s, acc):
            acc = list(acc)
            for j in range(lead_tiles + out_tiles):
                row = jnp.broadcast_to(signal[pl.ds(TILE * j + s, 1), :], (TILE, LANES))
                for i in range(max(0, j - lead_tiles), out_tiles):
                    off = TILE * (i + lead_tiles - j)
                    acc[i] = acc[i] + row * shifted[s, off : off + TILE]
            return tuple(acc)

        acc = lax.fori_loop(0, TILE, shift_body, tuple(acc))
        gated = jnp.concatenate(acc, 0) * q_ref[:, cols].astype(F32)
        gated_ref[:, cols] = gated
        squares[...] = squares[...] + gated * gated
        return 0

    lax.fori_loop(0, q_ref.shape[1] // LANES, group_body, 0)
    sums = lax.dot_general(
        jnp.ones((TILE, LANES), F32), squares[...], (((1,), (1,)), ((), ())),
        precision=lax.Precision.HIGHEST, preferred_element_type=F32,
    )
    for i in range(sums_ref.shape[0]):
        sums_ref[i] = sums


def norm_kernel(gated_ref, sums_ref, gain_ref, out_ref):
    total = sums_ref[0]
    for i in range(1, sums_ref.shape[0]):
        total = total + sums_ref[i]
    scale = jnp.transpose(lax.rsqrt(total / C + EPS))[:, 0:1]
    out_ref[...] = (gated_ref[...] * scale * gain_ref[...]).astype(BF16)


def shape(dims, dtype):
    return jax.ShapeDtypeStruct(dims, dtype)


def from_behind(block, axis):
    return lax.ppermute(block, axis, [(i - 1, i) for i in range(1, lax.axis_size(axis))])


def on_device(projected, short_filter, medium_filter, decay, residues, skip_gain, out_gain):
    _, row_count, chans = projected.shape
    ctx, ch = lax.axis_size("ctx"), lax.axis_size("ch")
    halo = from_behind(projected[:, row_count - 16 :], "ctx")
    reach = row_count + MED
    taps, reach_weights = pl.pallas_call(
        filter_kernel,
        out_shape=(shape((reach, chans), F32), shape((MODES, chans), F32)),
        scratch_shapes=[pltpu.VMEM((MED, LANES), F32), pltpu.VMEM((TILE, MED + TILE, LANES), F32)],
        compiler_params=PARAMS,
        name="filters",
    )(medium_filter, decay, residues, skip_gain[None])
    queries, product, tail, spread = pl.pallas_call(
        feature_kernel,
        out_shape=(
            shape((row_count, chans), BF16),
            shape((row_count, chans), BF16),
            shape((MED + MODES, chans), BF16),
            shape((ctx, MODES, chans), BF16),
        ),
        scratch_shapes=[pltpu.VMEM((3, row_count + TILE, LANES), F32)],
        compiler_params=PARAMS,
        name="features",
    )(projected, halo, short_filter, decay)
    tail = from_behind(tail, "ctx")
    states = lax.all_to_all(spread, "ctx", 0, 0, tiled=True)
    vmem = pl.BlockSpec(memory_space=pltpu.VMEM)
    gated, sums = pl.pallas_call(
        mix_kernel,
        out_shape=(shape((row_count, chans), F32), shape((ch, TILE, row_count), F32)),
        in_specs=[pl.BlockSpec(memory_space=pltpu.SMEM)] + [vmem] * 7,
        scratch_shapes=[
            pltpu.VMEM((TILE, reach + TILE, LANES), F32),
            pltpu.VMEM((reach, LANES), F32),
            pltpu.VMEM((row_count, LANES), F32),
        ],
        compiler_params=PARAMS,
        name="mix",
    )(lax.axis_index("ctx").reshape(1), taps, reach_weights, decay, states, tail, product, queries)
    sums = lax.all_to_all(sums, "ch", 0, 0, tiled=True)
    return pl.pallas_call(
        norm_kernel,
        out_shape=shape((row_count, chans), BF16),
        compiler_params=PARAMS,
        name="norm",
    )(gated, sums, out_gain[None])


def solution(mesh):
    in_specs = (
        P(None, "ctx", "ch"),
        P(None, None, "ch"),
        P(None, "ch"),
        P(None, "ch"),
        P(None, "ch"),
        P("ch"),
        P("ch"),
    )
    return jax.shard_map(on_device, mesh=mesh, in_specs=in_specs, out_specs=P("ctx", "ch"), check_vma=False)
```

time: 708 us -> 55.2 us (0.08); the launches traced: 696 us -> 54.3 us
  local copies, waits for them, and re-layouts: 594 us -> 3.26 us
  blocking collectives: 44.1 us -> 15.3 us
  matrix products: 27 us -> 0 us
  other arithmetic: 23.4 us -> 0 us
  Pallas kernels: 0 us -> 13.2 us
  starting transfers between devices: 6.69 us -> 16.6 us
    pad x3 -> x0, local copies, waits for them, and re-layouts: 378 us -> none  [on_device(): lax.associative_scan(compose, (jnp.broadcast_to(step_decay[None], summari...]
    unnamed x48 -> x15, local copies, waits for them, and re-layouts: 155 us -> 2.45 us
    all_gather x1 -> x0, blocking collectives: 27.9 us -> none  [on_device(): lax.all_gather(local_end[None].astype(jnp.bfloat16), 'ctx', axis=0, tiled...]
    dot_general x10 -> x0, matrix products: 27 us -> none  [the longest x7 16.3 us: wide_einsum(): return jnp.einsum(form, left, right, preferred_element_type=jnp.float32)]
    slice x11 -> x1, local copies, waits for them, and re-layouts: 22.5 us -> 0.81 us  [on_device(): halo = from_behind(projected[:, row_count - 16:], 'ctx')]
    psum x1 -> x0, blocking collectives: 16.3 us -> none  [on_device(): square_sum = lax.psum(jnp.sum(gated_out * gated_out, axis=1), 'ch')]
    all_to_all x0 -> x1, blocking collectives: none -> 15.3 us  [on_device(): sums = lax.all_to_all(sums, 'ch', 0, 0, tiled=True)]
    reshape x2 -> x0, local copies, waits for them, and re-layouts: 14.7 us -> none  [the longest x1 14 us: medium_conv(): band_table = jnp.dot(selector, medium_filter, preferred_element_type=jnp....]
  transfers between devices with their start and end apart: 2 -> 3, of which waited for: 1 -> 3; matrix products, arithmetic and copies ran while one was open for 8% -> 0% of each run, Pallas kernels for 0% -> 5%
where the time goes in v1:
time: 55.2 us; the launch traced here: 54.3 us
  starting transfers between devices  16.6 us (30%)
  blocking collectives  15.3 us (28%)
  Pallas kernels  13.2 us (24%)
  waiting for transfers between devices  5.81 us (11%)
  local copies, waits for them, and re-layouts  3.26 us (6%)
    all_to_all x1, blocking collectives, on_device(): sums = lax.all_to_all(sums, 'ch', 0, 0, tiled=True)  15.3 us
    all_to_all x1, starting transfers between devices, on_device(): states = lax.all_to_all(spread, 'ctx', 0, 0, tiled=True)  8.37 us
    ppermute x2, starting transfers between devices, from_behind(): lax.ppermute(block, axis, [(i - 1, i) for i in range(1, lax.axis_size(axi...  8.25 us
    pallas_call x1, Pallas kernels, on_device(): pl.pallas_call(mix_kernel, out_shape=(shape((row_count, chans), F32), sha...  7.29 us
    all_to_all x1, waiting for transfers between devices, on_device(): states = lax.all_to_all(spread, 'ctx', 0, 0, tiled=True)  3.27 us
    pallas_call x1, Pallas kernels, on_device(): pl.pallas_call(filter_kernel, out_shape=(shape((reach, chans), F32), shap...  2.69 us
    ppermute x2, waiting for transfers between devices, from_behind(): lax.ppermute(block, axis, [(i - 1, i) for i in range(1, lax.axis_size(axi...  2.54 us
    unnamed x15, local copies, waits for them, and re-layouts  2.45 us
  transfers between devices with their start and end apart: 3, of which 3 were waited for; matrix products, arithmetic and copies ran while one was open for 0% of the time, Pallas kernels for 5%

profile of v1, /device:TPU:1, one launch (start us, length us, event | category | flops | bytes accessed | tf_op | source)
XLA Modules:
  0.0 54.3 jit_solution(9827024449344591990)
XLA Ops:
  0.0 0.0 copy-start.6
  0.0 0.8 %slice.3 = bf16[3,16,512]{2,1,0:T(8,128)(2,1)S(1)} slice(bf16[3,192,512]{2,1,0:T(8,128)(2,1)} %proj_ref.1), slice={[0:3], [176:192], [0:512]} | slice | bytes 98304 | tf_op jit(solution)/shard_map/slice | solution.py:212
  0.8 0.0 copy-start.1
  0.8 4.7 %collective-permute-start = (bf16[3,16,512]{2,1,0:T(8,128)(2,1)S(1)}, bf16[3,16,512]{2,1,0:T(8,128)(2,1)S(1)}, u32[]{:S(2)}, u32[]{:S(2)}) collective-permute-start(bf16[3,16,512]{2,1,0:T(8,128)(2,1)S(1)} %slice.3), channel_id=1, source_target_pairs={{0,8},{8,16},{16,24},{24,32},{32,40},{40,48},{48,56},{56,64},{64,7... | collective-permute-start | bytes 147464 | tf_op jit(solution)/shard_map/ppermute | solution.py:206
  5.5 0.0 copy-done.6
  5.6 1.1 %collective-permute-done.halo_ref = bf16[3,16,512]{2,1,0:T(8,128)(2,1)S(1)} collective-permute-done((bf16[3,16,512]{2,1,0:T(8,128)(2,1)S(1)}, bf16[3,16,512]{2,1,0:T(8,128)(2,1)S(1)}, u32[]{:S(2)}, u32[]{:S(2)}) %collective-permute-start) | collective-permute-done | bytes 49184 | tf_op jit(solution)/shard_map/ppermute | solution.py:206
  6.7 0.0 copy-done.1
  6.7 0.0 copy-start
  6.7 1.1 %copy-done = bf16[3,192,512]{2,1,0:T(8,128)(2,1)S(1)} copy-done((bf16[3,192,512]{2,1,0:T(8,128)(2,1)S(1)}, bf16[3,192,512]{2,1,0:T(8,128)(2,1)}, u32[]{:S(2)}) %copy-start) | copy-done | bytes 589848
  7.8 2.3 %features.1 = (bf16[192,512]{1,0:T(8,128)(2,1)S(1)}, bf16[192,512]{1,0:T(8,128)(2,1)S(1)}, bf16[144,512]{1,0:T(8,128)(2,1)S(1)}, bf16[32,16,512]{2,1,0:T(8,128)(2,1)}) custom-call(bf16[3,192,512]{2,1,0:T(8,128)(2,1)S(1)} %copy-done, bf16[3,16,512]{2,1,0:T(8,128)(2,1)S(1)} %collective-permute-done.halo_ref, f32[7,3,512]{2,1,0:T(4,128)S(1)} %copy.8.short_ref, ...), custom_call_target="tpu_custom_call" | custom-call | tf_op jit(solution)/shard_map/features/pallas_call | solution.py:221
  10.1 0.0 copy-start.2
  10.1 0.0 copy-start.3
  10.1 8.4 %all-to-all-start = ((bf16[32,16,512]{2,1,0:T(8,128)(2,1)}), bf16[32,16,512]{2,1,0:T(8,128)(2,1)S(1)}, u32[]{:S(2)}, u32[]{:S(2)}) async-start(bf16[32,16,512]{2,1,0:T(8,128)(2,1)} %get-tuple-element.15), calls=%async_computation | async-start | bytes 1048576 | tf_op jit(solution)/shard_map/all_to_all | solution.py:234
  18.5 3.5 %collective-permute-start.1 = (bf16[144,512]{1,0:T(8,128)(2,1)S(1)}, bf16[144,512]{1,0:T(8,128)(2,1)S(1)}, u32[]{:S(2)}, u32[]{:S(2)}) collective-permute-start(bf16[144,512]{1,0:T(8,128)(2,1)S(1)} %get-tuple-element.16), channel_id=1, source_target_pairs={{0,8},{8,16},{16,24},{24,32},{32,40},{40,48},{48,56},{56,64},{64,7... | collective-permute-start | bytes 442376 | tf_op jit(solution)/shard_map/ppermute | solution.py:206
  22.0 0.0 copy-start.4
  22.0 0.0 copy-done.2
  22.0 0.0 copy-done.3
  22.1 0.7 %copy-done.4 = f32[512]{0:T(512)S(1)} copy-done((f32[512]{0:T(512)S(1)}, f32[512]{0:T(512)}, u32[]{:S(2)}) %copy-start.4) | copy-done | bytes 2072
  22.7 2.7 %filters.1 = (f32[320,512]{1,0:T(8,128)S(1)}, f32[16,512]{1,0:T(8,128)S(1)}) custom-call(bf16[128,512]{1,0:T(8,128)(2,1)S(1)} %copy-done.2, f32[16,512]{1,0:T(8,128)S(1)} %copy-done.1, f32[16,512]{1,0:T(8,128)S(1)} %copy-done.3, f32[1,512]{1,0:T(1,128)S(1)} %bitcast.3), custom_call_target="tpu_custom_call" | custom-call | tf_op jit(solution)/shard_map/filters/pallas_call | solution.py:214
  25.4 1.4 %collective-permute-done.1.tail_ref = bf16[144,512]{1,0:T(8,128)(2,1)S(1)} collective-permute-done((bf16[144,512]{1,0:T(8,128)(2,1)S(1)}, bf16[144,512]{1,0:T(8,128)(2,1)S(1)}, u32[]{:S(2)}, u32[]{:S(2)}) %collective-permute-start.1) | collective-permute-done | bytes 147488 | tf_op jit(solution)/shard_map/ppermute | solution.py:206
  26.8 3.3 %all-to-all-done.states_ref = bf16[32,16,512]{2,1,0:T(8,128)(2,1)S(1)} async-done(((bf16[32,16,512]{2,1,0:T(8,128)(2,1)}), bf16[32,16,512]{2,1,0:T(8,128)(2,1)S(1)}, u32[]{:S(2)}, u32[]{:S(2)}) %all-to-all-start) | async-done | bytes 524320 | tf_op jit(solution)/shard_map/all_to_all | solution.py:234
  30.1 7.3 %mix.1 = (f32[192,512]{1,0:T(8,128)S(1)}, f32[8,8,192]{2,1,0:T(8,128)S(1)}) custom-call(s32[1]{0:T(128)} %bitcast.index_ref, f32[320,512]{1,0:T(8,128)S(1)} %get-tuple-element.13.g_ref, f32[16,512]{1,0:T(8,128)S(1)} %get-tuple-element.14.wm_ref, f32[16,512]{1,0:T(8,128)S(1)} %copy-done.1, bf16[32,16,512]{2,1,0:T(8,128)(2,1)S(1)} %all-to-all-done.states_ref, ...), custom_call_target="tpu_custom_call" | custom-call | tf_op jit(solution)/shard_map/mix/pallas_call | solution.py:236
  37.4 15.3 %all_to_all.10.sums_ref = f32[8,8,192]{2,1,0:T(8,128)S(1)} all-to-all(f32[8,8,192]{2,1,0:T(8,128)S(1)} %get-tuple-element.20), channel_id=1, replica_groups=mesh['ctx'=32,'ch'=8] {'ch'}, dimensions={0} | all-to-all | bytes 98304 | tf_op jit(solution)/shard_map/all_to_all | solution.py:248
  52.7 0.0 copy-start.5
  52.7 0.7 %copy-done.5 = f32[512]{0:T(512)S(1)} copy-done((f32[512]{0:T(512)S(1)}, f32[512]{0:T(512)}, u32[]{:S(2)}) %copy-start.5) | copy-done | bytes 2072
  53.3 0.9 %norm.1 = bf16[192,512]{1,0:T(8,128)(2,1)} custom-call(f32[192,512]{1,0:T(8,128)S(1)} %get-tuple-element.19.gated_ref, f32[8,8,192]{2,1,0:T(8,128)S(1)} %all_to_all.10.sums_ref, f32[1,512]{1,0:T(1,128)S(1)} %bitcast.4), custom_call_target="tpu_custom_call" | custom-call | tf_op jit(solution)/shard_map/norm/pallas_call | solution.py:249
  (1 shorter events, 0.0 us)
Async XLA Ops:
  0.0 5.5 %copy-start.6 = (f32[7,3,512]{2,0,1:T(8,128)S(1)}, f32[7,3,512]{2,0,1:T(8,128)}, u32[]{:S(2)}) copy-start(f32[7,3,512]{2,0,1:T(8,128)} %param.8) | copy-start | bytes 129028
  0.8 5.9 %copy-start.1 = (f32[16,512]{1,0:T(8,128)S(1)}, f32[16,512]{1,0:T(8,128)}, u32[]{:S(2)}) copy-start(f32[16,512]{1,0:T(8,128)} %decay_ref.5) | copy-start | bytes 98308
  0.8 5.9 %collective-permute-start = (bf16[3,16,512]{2,1,0:T(8,128)(2,1)S(1)}, bf16[3,16,512]{2,1,0:T(8,128)(2,1)S(1)}, u32[]{:S(2)}, u32[]{:S(2)}) collective-permute-start(bf16[3,16,512]{2,1,0:T(8,128)(2,1)S(1)} %slice.3), channel_id=1, source_target_pairs={{0,8},{8,16},{16,24},{24,32},{32,40},{40,48},{48,56},{56,64},{64,7... | collective-permute-start | bytes 147464 | tf_op jit(solution)/shard_map/ppermute | solution.py:206
  6.7 1.1 %copy-start = (bf16[3,192,512]{2,1,0:T(8,128)(2,1)S(1)}, bf16[3,192,512]{2,1,0:T(8,128)(2,1)}, u32[]{:S(2)}) copy-start(bf16[3,192,512]{2,1,0:T(8,128)(2,1)} %proj_ref.1) | copy-start | bytes 1769476
  10.1 12.0 %copy-start.2 = (bf16[128,512]{1,0:T(8,128)(2,1)S(1)}, bf16[128,512]{1,0:T(8,128)(2,1)}, u32[]{:S(2)}) copy-start(bf16[128,512]{1,0:T(8,128)(2,1)} %med_ref.1) | copy-start | bytes 393220
  10.1 12.0 %copy-start.3 = (f32[16,512]{1,0:T(8,128)S(1)}, f32[16,512]{1,0:T(8,128)}, u32[]{:S(2)}) copy-start(f32[16,512]{1,0:T(8,128)} %res_ref.1) | copy-start | bytes 98308
  10.1 20.0 %all-to-all-start = ((bf16[32,16,512]{2,1,0:T(8,128)(2,1)}), bf16[32,16,512]{2,1,0:T(8,128)(2,1)S(1)}, u32[]{:S(2)}, u32[]{:S(2)}) async-start(bf16[32,16,512]{2,1,0:T(8,128)(2,1)} %get-tuple-element.15), calls=%async_computation | async-start | bytes 1048576 | tf_op jit(solution)/shard_map/all_to_all | solution.py:234
  18.5 8.4 %collective-permute-start.1 = (bf16[144,512]{1,0:T(8,128)(2,1)S(1)}, bf16[144,512]{1,0:T(8,128)(2,1)S(1)}, u32[]{:S(2)}, u32[]{:S(2)}) collective-permute-start(bf16[144,512]{1,0:T(8,128)(2,1)S(1)} %get-tuple-element.16), channel_id=1, source_target_pairs={{0,8},{8,16},{16,24},{24,32},{32,40},{40,48},{48,56},{56,64},{64,7... | collective-permute-start | bytes 442376 | tf_op jit(solution)/shard_map/ppermute | solution.py:206
  22.0 0.7 %copy-start.4 = (f32[512]{0:T(512)S(1)}, f32[512]{0:T(512)}, u32[]{:S(2)}) copy-start(f32[512]{0:T(512)} %param.12) | copy-start | bytes 6148
  52.7 0.7 %copy-start.5 = (f32[512]{0:T(512)S(1)}, f32[512]{0:T(512)}, u32[]{:S(2)}) copy-start(f32[512]{0:T(512)} %param.13) | copy-start | bytes 6148

commit v2 on v1

--- a/solution.py
+++ b/solution.py
@@ -1,4 +1,3 @@
-import functools
 import jax
 import jax.numpy as jnp
 from jax import lax
@@ -88,7 +87,7 @@
     lax.fori_loop(0, g_ref.shape[1] // LANES, group_body, 0)
 
 
-def feature_kernel(proj_ref, halo_ref, short_ref, decay_ref, q_ref, p_ref, tail_ref, spread_ref, ext):
+def feature_kernel(proj_ref, halo_ref, short_ref, decay_ref, after_ref, q_ref, p_ref, tail_ref, spread_ref, ext):
     row_count = proj_ref.shape[1]
     all_tiles = row_count // TILE
     part_tiles = all_tiles - MED // TILE
@@ -100,9 +99,9 @@
         for j in range(3):
             ext[j, 0:TILE] = halo_ref[j, :, cols].astype(F32)[TILE : 2 * TILE]
             ext[j, TILE : TILE + row_count] = proj_ref[j, :, cols].astype(F32)
-            total = short_ref[0, j : j + 1, cols] * ext[j, TILE : TILE + row_count]
+            total = short_ref[j, 0:1, cols] * ext[j, TILE : TILE + row_count]
             for d in range(1, SHORT):
-                total = total + short_ref[d, j : j + 1, cols] * ext[j, TILE - d : TILE - d + row_count]
+                total = total + short_ref[j, d : d + 1, cols] * ext[j, TILE - d : TILE - d + row_count]
             feats.append(total.astype(BF16))
         q_ref[:, cols] = feats[0]
         product = (feats[1].astype(F32) * feats[2].astype(F32)).astype(BF16)
@@ -130,41 +129,19 @@
     lax.fori_loop(0, q_ref.shape[1] // LANES, group_body, 0)
 
 
-def mix_kernel(index_ref, g_ref, wm_ref, decay_ref, states_ref, tail_ref, p_ref, q_ref, gated_ref, sums_ref,
-               shifted, signal, squares):
+def direct_kernel(g_ref, tail_ref, p_ref, near_ref, shifted, signal):
     row_count = p_ref.shape[0]
     out_tiles = row_count // TILE
     lead_tiles = MED // TILE
     reach = g_ref.shape[0]
-    own = index_ref[0]
-    squares[...] = jnp.zeros(squares.shape, F32)
-
-    def group_body(group, _):
-        cols = lanes_of(group)
-        rows = row_iota()
+
+    def group_body(group, _):
+        cols = lanes_of(group)
         for s in range(TILE):
             shifted[s, 0:TILE] = jnp.zeros((TILE, LANES), F32)
             shifted[s, s : s + reach] = g_ref[:, cols]
-        tail = tail_ref[:, cols].astype(F32)
-        signal[0:MED] = tail[0:MED]
+        signal[0:MED] = tail_ref[0:MED, cols].astype(F32)
         signal[MED : MED + row_count] = p_ref[:, cols].astype(F32)
-        decay = decay_ref[:, cols]
-        span = jnp.exp(-float(row_count) * decay)
-
-        def carry_body(j, carried):
-            return carried * span + states_ref[j, :, cols].astype(F32)
-
-        carried = lax.fori_loop(0, own - 1, carry_body, jnp.zeros((MODES, LANES), F32))
-        carried = tail[MED : MED + MODES] + jnp.exp(-float(row_count - MED) * decay) * carried
-        carried = carried * wm_ref[:, cols]
-        eight = jnp.exp(-TILE * decay)
-        acc = [jnp.zeros((TILE, LANES), F32) for _ in range(out_tiles)]
-        for n in range(MODES):
-            step = jnp.broadcast_to(eight[n : n + 1], (TILE, LANES))
-            term = carried[n : n + 1] * jnp.exp(-decay[n : n + 1] * (rows + 2))
-            for i in range(out_tiles):
-                acc[i] = acc[i] + term
-                term = term * step
 
         def shift_body(s, acc):
             acc = list(acc)
@@ -175,7 +152,39 @@
                     acc[i] = acc[i] + row * shifted[s, off : off + TILE]
             return tuple(acc)
 
-        acc = lax.fori_loop(0, TILE, shift_body, tuple(acc))
+        acc = lax.fori_loop(0, TILE, shift_body, tuple(jnp.zeros((TILE, LANES), F32) for _ in range(out_tiles)))
+        near_ref[:, cols] = jnp.concatenate(acc, 0)
+        return 0
+
+    lax.fori_loop(0, p_ref.shape[1] // LANES, group_body, 0)
+
+
+def combine_kernel(index_ref, wm_ref, decay_ref, states_ref, tail_ref, near_ref, q_ref, gated_ref, sums_ref,
+                   entry, squares):
+    row_count = q_ref.shape[0]
+    out_tiles = row_count // TILE
+    squares[...] = jnp.zeros(squares.shape, F32)
+    span = jnp.exp(-float(row_count) * decay_ref[...])
+
+    def carry_body(j, carried):
+        return carried * span + states_ref[j].astype(F32)
+
+    carried = lax.fori_loop(0, index_ref[0] - 1, carry_body, jnp.zeros(span.shape, F32))
+    carried = tail_ref[MED : MED + MODES].astype(F32) + jnp.exp(-float(row_count - MED) * decay_ref[...]) * carried
+    entry[...] = carried * wm_ref[...]
+
+    def group_body(group, _):
+        cols = lanes_of(group)
+        rows = row_iota()
+        decay = decay_ref[:, cols]
+        eight = jnp.exp(-TILE * decay)
+        acc = tiles_of(near_ref[:, cols])
+        for n in range(MODES):
+            step = jnp.broadcast_to(eight[n : n + 1], (TILE, LANES))
+            term = entry[n : n + 1, cols] * jnp.exp(-decay[n : n + 1] * (rows + 2))
+            for i in range(out_tiles):
+                acc[i] = acc[i] + term
+                term = term * step
         gated = jnp.concatenate(acc, 0) * q_ref[:, cols].astype(F32)
         gated_ref[:, cols] = gated
         squares[...] = squares[...] + gated * gated
@@ -211,6 +220,7 @@
     ctx, ch = lax.axis_size("ctx"), lax.axis_size("ch")
     halo = from_behind(projected[:, row_count - 16 :], "ctx")
     reach = row_count + MED
+    vmem = pl.BlockSpec(memory_space=pltpu.VMEM)
     taps, reach_weights = pl.pallas_call(
         filter_kernel,
         out_shape=(shape((reach, chans), F32), shape((MODES, chans), F32)),
@@ -226,25 +236,28 @@
             shape((MED + MODES, chans), BF16),
             shape((ctx, MODES, chans), BF16),
         ),
+        in_specs=[vmem] * 4 + [pl.BlockSpec(memory_space=pl.ANY)],
         scratch_shapes=[pltpu.VMEM((3, row_count + TILE, LANES), F32)],
         compiler_params=PARAMS,
         name="features",
-    )(projected, halo, short_filter, decay)
+    )(projected, halo, jnp.transpose(short_filter, (1, 0, 2)), decay, reach_weights)
     tail = from_behind(tail, "ctx")
     states = lax.all_to_all(spread, "ctx", 0, 0, tiled=True)
-    vmem = pl.BlockSpec(memory_space=pltpu.VMEM)
+    near = pl.pallas_call(
+        direct_kernel,
+        out_shape=shape((row_count, chans), F32),
+        scratch_shapes=[pltpu.VMEM((TILE, reach + TILE, LANES), F32), pltpu.VMEM((reach, LANES), F32)],
+        compiler_params=PARAMS,
+        name="direct",
+    )(taps, tail, product)
     gated, sums = pl.pallas_call(
-        mix_kernel,
+        combine_kernel,
         out_shape=(shape((row_count, chans), F32), shape((ch, TILE, row_count), F32)),
-        in_specs=[pl.BlockSpec(memory_space=pltpu.SMEM)] + [vmem] * 7,
-        scratch_shapes=[
-            pltpu.VMEM((TILE, reach + TILE, LANES), F32),
-            pltpu.VMEM((reach, LANES), F32),
-            pltpu.VMEM((row_count, LANES), F32),
-        ],
-        compiler_params=PARAMS,
-        name="mix",
-    )(lax.axis_index("ctx").reshape(1), taps, reach_weights, decay, states, tail, product, queries)
+        in_specs=[pl.BlockSpec(memory_space=pltpu.SMEM)] + [vmem] * 6,
+        scratch_shapes=[pltpu.VMEM((MODES, chans), F32), pltpu.VMEM((row_count, LANES), F32)],
+        compiler_params=PARAMS,
+        name="combine",
+    )(lax.axis_index("ctx").reshape(1), reach_weights, decay, states, tail, near, queries)
     sums = lax.all_to_all(sums, "ch", 0, 0, tiled=True)
     return pl.pallas_call(
         norm_kernel,

time: 55.2 us -> 56 us (1.014)
  the two profiles are of different devices: /device:TPU:1 before, /device:TPU:2 now
where the time goes in v2:
time: 56 us; the launch traced here: 55.6 us
  blocking collectives  16.7 us (30%)
  Pallas kernels  13.2 us (24%)
  waiting for transfers between devices  11.5 us (21%)
  starting transfers between devices  10.6 us (19%)
  local copies, waits for them, and re-layouts  3.5 us (6%)
    all_to_all x1, blocking collectives, on_device(): sums = lax.all_to_all(sums, 'ch', 0, 0, tiled=True)  16.7 us
    ppermute x2, waiting for transfers between devices, from_behind(): lax.ppermute(block, axis, [(i - 1, i) for i in range(1, lax.axis_size(axi...  11.5 us
    all_to_all x1, starting transfers between devices, on_device(): states = lax.all_to_all(spread, 'ctx', 0, 0, tiled=True)  6.68 us
    pallas_call x1, Pallas kernels, on_device(): pl.pallas_call(direct_kernel, out_shape=shape((row_count, chans), F32), s...  6.46 us
    ppermute x2, starting transfers between devices, from_behind(): lax.ppermute(block, axis, [(i - 1, i) for i in range(1, lax.axis_size(axi...  3.97 us
    pallas_call x1, Pallas kernels, on_device(): pl.pallas_call(filter_kernel, out_shape=(shape((reach, chans), F32), shap...  2.69 us
    unnamed x14, local copies, waits for them, and re-layouts  2.66 us
    pallas_call x1, Pallas kernels, on_device(): pl.pallas_call(feature_kernel, out_shape=(shape((row_count, chans), BF16)...  2.3 us
  transfers between devices with their start and end apart: 3, of which 2 were waited for; matrix products, arithmetic and copies ran while one was open for 0% of the time, Pallas kernels for 16%

profile of v2, /device:TPU:2, one launch (start us, length us, event | category | flops | bytes accessed | tf_op | source)
XLA Modules:
  0.0 55.6 jit_solution(198149624566059834)
XLA Ops:
  0.0 0.0 copy-start.1
  0.0 0.0 copy-start.4
  0.0 0.0 copy-start.5
  0.0 0.8 %slice.3 = bf16[3,16,512]{2,1,0:T(8,128)(2,1)S(1)} slice(bf16[3,192,512]{2,1,0:T(8,128)(2,1)} %proj_ref.1), slice={[0:3], [176:192], [0:512]} | slice | bytes 98304 | tf_op jit(solution)/shard_map/slice | solution.py:221
  0.9 1.9 %collective-permute-start = (bf16[3,16,512]{2,1,0:T(8,128)(2,1)S(1)}, bf16[3,16,512]{2,1,0:T(8,128)(2,1)S(1)}, u32[]{:S(2)}, u32[]{:S(2)}) collective-permute-start(bf16[3,16,512]{2,1,0:T(8,128)(2,1)S(1)} %slice.3), channel_id=1, source_target_pairs={{0,8},{8,16},{16,24},{24,32},{32,40},{40,48},{48,56},{56,64},{64,7... | collective-permute-start | bytes 147464 | tf_op jit(solution)/shard_map/ppermute | solution.py:215
  2.8 0.0 copy-done.1
  2.8 0.0 copy-done.4
  2.8 0.0 copy-done.5
  2.8 0.0 copy-start.2
  2.8 0.9 %copy-done.2 = bf16[128,512]{1,0:T(8,128)(2,1)S(1)} copy-done((bf16[128,512]{1,0:T(8,128)(2,1)S(1)}, bf16[128,512]{1,0:T(8,128)(2,1)}, u32[]{:S(2)}) %copy-start.2) | copy-done | bytes 131096
  3.7 0.0 copy-start.3
  3.7 2.7 %filters.1 = (f32[320,512]{1,0:T(8,128)S(1)}, f32[16,512]{1,0:T(8,128)S(1)}) custom-call(bf16[128,512]{1,0:T(8,128)(2,1)S(1)} %copy-done.2, f32[16,512]{1,0:T(8,128)S(1)} %copy-done.1, f32[16,512]{1,0:T(8,128)S(1)} %copy-done.4, f32[1,512]{1,0:T(1,128)S(1)} %bitcast.5), custom_call_target="tpu_custom_call" | custom-call | tf_op jit(solution)/shard_map/filters/pallas_call | solution.py:224
  6.4 2.0 %collective-permute-done.halo_ref = bf16[3,16,512]{2,1,0:T(8,128)(2,1)S(1)} collective-permute-done((bf16[3,16,512]{2,1,0:T(8,128)(2,1)S(1)}, bf16[3,16,512]{2,1,0:T(8,128)(2,1)S(1)}, u32[]{:S(2)}, u32[]{:S(2)}) %collective-permute-start) | collective-permute-done | bytes 49184 | tf_op jit(solution)/shard_map/ppermute | solution.py:215
  8.4 0.0 copy-done.3
  8.4 0.0 copy-start
  8.4 1.1 %copy-done = bf16[3,192,512]{2,1,0:T(8,128)(2,1)S(1)} copy-done((bf16[3,192,512]{2,1,0:T(8,128)(2,1)S(1)}, bf16[3,192,512]{2,1,0:T(8,128)(2,1)}, u32[]{:S(2)}) %copy-start) | copy-done | bytes 589848
  9.4 2.3 %features.1 = (bf16[192,512]{1,0:T(8,128)(2,1)S(1)}, bf16[192,512]{1,0:T(8,128)(2,1)S(1)}, bf16[144,512]{1,0:T(8,128)(2,1)S(1)}, bf16[32,16,512]{2,1,0:T(8,128)(2,1)}) custom-call(bf16[3,192,512]{2,1,0:T(8,128)(2,1)S(1)} %copy-done, bf16[3,16,512]{2,1,0:T(8,128)(2,1)S(1)} %collective-permute-done.halo_ref, f32[3,7,512]{2,1,0:T(8,128)S(1)} %bitcast.4, ...), custom_call_target="tpu_custom_call" | custom-call | tf_op jit(solution)/shard_map/features/pallas_call | solution.py:231
  11.7 6.7 %all-to-all-start = ((bf16[32,16,512]{2,1,0:T(8,128)(2,1)}), bf16[32,16,512]{2,1,0:T(8,128)(2,1)S(1)}, u32[]{:S(2)}, u32[]{:S(2)}) async-start(bf16[32,16,512]{2,1,0:T(8,128)(2,1)} %get-tuple-element.14), calls=%async_computation | async-start | bytes 1048576 | tf_op jit(solution)/shard_map/all_to_all | solution.py:245
  18.4 2.1 %collective-permute-start.1 = (bf16[144,512]{1,0:T(8,128)(2,1)S(1)}, bf16[144,512]{1,0:T(8,128)(2,1)S(1)}, u32[]{:S(2)}, u32[]{:S(2)}) collective-permute-start(bf16[144,512]{1,0:T(8,128)(2,1)S(1)} %get-tuple-element.15), channel_id=1, source_target_pairs={{0,8},{8,16},{16,24},{24,32},{32,40},{40,48},{48,56},{56,64},{64,7... | collective-permute-start | bytes 442376 | tf_op jit(solution)/shard_map/ppermute | solution.py:215
  20.5 9.5 %collective-permute-done.1.tail_ref = bf16[144,512]{1,0:T(8,128)(2,1)S(1)} collective-permute-done((bf16[144,512]{1,0:T(8,128)(2,1)S(1)}, bf16[144,512]{1,0:T(8,128)(2,1)S(1)}, u32[]{:S(2)}, u32[]{:S(2)}) %collective-permute-start.1) | collective-permute-done | bytes 147488 | tf_op jit(solution)/shard_map/ppermute | solution.py:215
  30.0 6.5 %direct.1.near_ref = f32[192,512]{1,0:T(8,128)S(1)} custom-call(f32[320,512]{1,0:T(8,128)S(1)} %get-tuple-element.16.g_ref, bf16[144,512]{1,0:T(8,128)(2,1)S(1)} %collective-permute-done.1.tail_ref, bf16[192,512]{1,0:T(8,128)(2,1)S(1)} %get-tuple-element.17.p_ref), custom_call_target="tpu_custom_call" | custom-call | tf_op jit(solution)/shard_map/direct/pallas_call | solution.py:246
  36.5 0.0 all-to-all-done.states_ref
  36.5 0.9 %combine.1 = (f32[192,512]{1,0:T(8,128)S(1)}, f32[8,8,192]{2,1,0:T(8,128)S(1)}) custom-call(s32[1]{0:T(128)} %bitcast.index_ref, f32[16,512]{1,0:T(8,128)S(1)} %get-tuple-element.13.after_ref.wm_ref, f32[16,512]{1,0:T(8,128)S(1)} %copy-done.1, bf16[32,16,512]{2,1,0:T(8,128)(2,1)S(1)} %all-to-all-done.states_ref, ...), custom_call_target="tpu_custom_call" | custom-call | tf_op jit(solution)/shard_map/combine/pallas_call | solution.py:253
  37.3 16.7 %all_to_all.10.sums_ref = f32[8,8,192]{2,1,0:T(8,128)S(1)} all-to-all(f32[8,8,192]{2,1,0:T(8,128)S(1)} %get-tuple-element.20), channel_id=1, replica_groups=mesh['ctx'=32,'ch'=8] {'ch'}, dimensions={0} | all-to-all | bytes 98304 | tf_op jit(solution)/shard_map/all_to_all | solution.py:261
  54.0 0.0 copy-start.6
  54.0 0.7 %copy-done.6 = f32[512]{0:T(512)S(1)} copy-done((f32[512]{0:T(512)S(1)}, f32[512]{0:T(512)}, u32[]{:S(2)}) %copy-start.6) | copy-done | bytes 2072
  54.7 0.9 %norm.1 = bf16[192,512]{1,0:T(8,128)(2,1)} custom-call(f32[192,512]{1,0:T(8,128)S(1)} %get-tuple-element.19.gated_ref, f32[8,8,192]{2,1,0:T(8,128)S(1)} %all_to_all.10.sums_ref, f32[1,512]{1,0:T(1,128)S(1)} %bitcast.6), custom_call_target="tpu_custom_call" | custom-call | tf_op jit(solution)/shard_map/norm/pallas_call | solution.py:262
Async XLA Ops:
  0.0 2.8 %copy-start.1 = (f32[16,512]{1,0:T(8,128)S(1)}, f32[16,512]{1,0:T(8,128)}, u32[]{:S(2)}) copy-start(f32[16,512]{1,0:T(8,128)} %decay_ref.5) | copy-start | bytes 98308
  0.0 2.8 %copy-start.4 = (f32[16,512]{1,0:T(8,128)S(1)}, f32[16,512]{1,0:T(8,128)}, u32[]{:S(2)}) copy-start(f32[16,512]{1,0:T(8,128)} %res_ref.1) | copy-start | bytes 98308
  0.0 2.8 %copy-start.5 = (f32[512]{0:T(512)S(1)}, f32[512]{0:T(512)}, u32[]{:S(2)}) copy-start(f32[512]{0:T(512)} %param.12) | copy-start | bytes 6148
  0.9 7.5 %collective-permute-start = (bf16[3,16,512]{2,1,0:T(8,128)(2,1)S(1)}, bf16[3,16,512]{2,1,0:T(8,128)(2,1)S(1)}, u32[]{:S(2)}, u32[]{:S(2)}) collective-permute-start(bf16[3,16,512]{2,1,0:T(8,128)(2,1)S(1)} %slice.3), channel_id=1, source_target_pairs={{0,8},{8,16},{16,24},{24,32},{32,40},{40,48},{48,56},{56,64},{64,7... | collective-permute-start | bytes 147464 | tf_op jit(solution)/shard_map/ppermute | solution.py:215
  2.8 0.9 %copy-start.2 = (bf16[128,512]{1,0:T(8,128)(2,1)S(1)}, bf16[128,512]{1,0:T(8,128)(2,1)}, u32[]{:S(2)}) copy-start(bf16[128,512]{1,0:T(8,128)(2,1)} %med_ref.1) | copy-start | bytes 393220
  3.7 4.7 %copy-start.3 = (f32[7,3,512]{2,0,1:T(8,128)S(1)}, f32[7,3,512]{2,0,1:T(8,128)}, u32[]{:S(2)}) copy-start(f32[7,3,512]{2,0,1:T(8,128)} %param.8) | copy-start | bytes 129028
  8.4 1.1 %copy-start = (bf16[3,192,512]{2,1,0:T(8,128)(2,1)S(1)}, bf16[3,192,512]{2,1,0:T(8,128)(2,1)}, u32[]{:S(2)}) copy-start(bf16[3,192,512]{2,1,0:T(8,128)(2,1)} %proj_ref.1) | copy-start | bytes 1769476
  11.7 24.7 %all-to-all-start = ((bf16[32,16,512]{2,1,0:T(8,128)(2,1)}), bf16[32,16,512]{2,1,0:T(8,128)(2,1)S(1)}, u32[]{:S(2)}, u32[]{:S(2)}) async-start(bf16[32,16,512]{2,1,0:T(8,128)(2,1)} %get-tuple-element.14), calls=%async_computation | async-start | bytes 1048576 | tf_op jit(solution)/shard_map/all_to_all | solution.py:245
  18.4 11.6 %collective-permute-start.1 = (bf16[144,512]{1,0:T(8,128)(2,1)S(1)}, bf16[144,512]{1,0:T(8,128)(2,1)S(1)}, u32[]{:S(2)}, u32[]{:S(2)}) collective-permute-start(bf16[144,512]{1,0:T(8,128)(2,1)S(1)} %get-tuple-element.15), channel_id=1, source_target_pairs={{0,8},{8,16},{16,24},{24,32},{32,40},{40,48},{48,56},{56,64},{64,7... | collective-permute-start | bytes 442376 | tf_op jit(solution)/shard_map/ppermute | solution.py:215
  54.0 0.7 %copy-start.6 = (f32[512]{0:T(512)S(1)}, f32[512]{0:T(512)}, u32[]{:S(2)}) copy-start(f32[512]{0:T(512)} %param.13) | copy-start | bytes 6148

commit v3 on v2

v3 whole, which is shorter than its diff:
```python
import functools
import jax
import jax.numpy as jnp
from jax import lax
from jax.experimental import pallas as pl
from jax.experimental.pallas import tpu as pltpu
from jax.sharding import PartitionSpec as P

C = 4096
SHORT = 7
MED = 128
MODES = 16
EPS = 1e-06
LANES = 128
TILE = 8
EDGE = 16
BLOCK = 64
F32 = jnp.float32
BF16 = jnp.bfloat16
PARAMS = pltpu.CompilerParams(vmem_limit_bytes=48 * 1024 * 1024)


def row_iota():
    return lax.broadcasted_iota(jnp.int32, (TILE, LANES), 0).astype(F32)


def lanes_of(group):
    return pl.ds(pl.multiple_of(group * LANES, LANES), LANES)


def one_minus_exp(x):
    return x * (1 - x * (1 / 2) * (1 - x * (1 / 3) * (1 - x * (1 / 4) * (1 - x * (1 / 5) * (1 - x * (1 / 6))))))


def tiles_of(array):
    return [array[TILE * i : TILE * (i + 1)] for i in range(array.shape[0] // TILE)]


def modal_sums(tiles, decay, rows):
    eight = jnp.exp(-TILE * decay)
    sums = []
    for n in range(MODES):
        step = jnp.broadcast_to(eight[n : n + 1], (TILE, LANES))
        state = tiles[0]
        for tile in tiles[1:]:
            state = state * step + tile
        sums.append(jnp.sum(state * jnp.exp(-decay[n : n + 1] * (TILE - 1 - rows)), axis=0, keepdims=True))
    return jnp.concatenate(sums, 0)


def feature_kernel(proj_ref, short_ref, *refs):
    params, (q_ref, p_ref, edge_ref, head_ref), copies, (ext,) = refs[:5], refs[5:9], refs[9:14], refs[14:]
    row_count = proj_ref.shape[1]

    def group_body(group, _):
        cols = lanes_of(group)
        feats = []
        for j in range(3):
            raw = proj_ref[j, :, cols]
            edge_ref[EDGE * j : EDGE * (j + 1), cols] = raw[row_count - EDGE :]
            ext[j, 0:TILE] = jnp.zeros((TILE, LANES), F32)
            ext[j, TILE : TILE + row_count] = raw.astype(F32)
            total = short_ref[j, 0:1, cols] * ext[j, TILE : TILE + row_count]
            for d in range(1, SHORT):
                total = total + short_ref[j, d : d + 1, cols] * ext[j, TILE - d : TILE - d + row_count]
            head_ref[j, :, cols] = total[0:TILE]
            feats.append(total.astype(BF16))
        q_ref[:, cols] = feats[0]
        product = (feats[1].astype(F32) * feats[2].astype(F32)).astype(BF16)
        p_ref[:, cols] = product
        edge_ref[3 * EDGE : 3 * EDGE + MED, cols] = product[row_count - MED :]
        return 0

    lax.fori_loop(0, q_ref.shape[1] // LANES, group_body, 0)
    for param, copied in zip(params, copies):
        copied[...] = param[...]


def table_kernel(p_ref, med_ref, decay_ref, res_ref, skip_ref, g_ref, wm_ref, sums_ref, med_f32, shifted):
    med_tiles = MED // TILE
    far_tiles = g_ref.shape[0] // TILE - med_tiles
    part_tiles = (p_ref.shape[0] - MED) // TILE

    def group_body(group, _):
        cols = lanes_of(group)
        rows = row_iota()
        decay = decay_ref[:, cols]
        weights = res_ref[:, cols] * jnp.sqrt(one_minus_exp(2.0 * decay))
        eight = jnp.exp(-TILE * decay)
        med = med_ref[:, cols].astype(F32)
        med_f32[...] = med
        product = tiles_of(p_ref[:, cols].astype(F32))
        near = [jnp.zeros((TILE, LANES), F32) for _ in range(med_tiles)]
        far = [jnp.zeros((TILE, LANES), F32) for _ in range(far_tiles)]
        for n in range(MODES):
            rate = decay[n : n + 1]
            step = jnp.broadcast_to(eight[n : n + 1], (TILE, LANES))
            weight = weights[n : n + 1]
            powers = jnp.exp(-rate * rows)
            close = jnp.exp(-rate * (TILE - 1 - rows))
            term = weight * powers
            state = jnp.zeros((TILE, LANES), F32)
            for i in range(med_tiles):
                near[i] = near[i] + term
                term = term * step
                state = state * step + med[TILE * i : TILE * (i + 1)]
            reach = jnp.sum(state * close, axis=0, keepdims=True) * weight
            wm_ref[n : n + 1, cols] = reach
            term = reach * jnp.exp(-rate * (rows + 1))
            for i in range(far_tiles):
                far[i] = far[i] + term
                term = term * step
            state = product[1]
            for i in range(2, len(product)):
                if i == part_tiles:
                    sums_ref[1, n : n + 1, cols] = jnp.sum(state * close, axis=0, keepdims=True)
                state = state * step + product[i]
            sums_ref[0, n : n + 1, cols] = jnp.sum(state * close, axis=0, keepdims=True)
        near[0] = near[0] + jnp.where(rows == 0, skip_ref[:, cols], 0.0)
        taps = jnp.concatenate(near, 0)
        for s in range(TILE):
            shifted[s, 0:TILE] = jnp.zeros((TILE, LANES), F32)
            shifted[s, s : s + MED] = taps

        def shift_body(s, acc):
            acc = list(acc)
            bank = [shifted[s, TILE * i : TILE * (i + 1)] for i in range(med_tiles)]
            for j in range(med_tiles):
                row = jnp.broadcast_to(med_f32[pl.ds(TILE * j + s, 1), :], (TILE, LANES))
                for i in range(j, med_tiles):
                    acc[i] = acc[i] + row * bank[i - j]
            return tuple(acc)

        acc = lax.fori_loop(0, TILE, shift_body, tuple(jnp.zeros((TILE, LANES), F32) for _ in range(med_tiles)))
        g_ref[:, cols] = jnp.concatenate(list(acc) + far, 0)
        return 0

    lax.fori_loop(0, g_ref.shape[1] // LANES, group_body, 0)


def first_kernel(edge_ref, head_ref, short_ref, decay_ref, sums_ref, spread_ref, part_ref, first_ref, ext, *, row_count):
    def group_body(group, _):
        cols = lanes_of(group)
        feats = []
        for j in range(3):
            before = edge_ref[EDGE * j : EDGE * (j + 1), cols].astype(F32)
            ext[j, 0:TILE] = before[EDGE - TILE :]
            ext[j, TILE : 2 * TILE] = jnp.zeros((TILE, LANES), F32)
            total = head_ref[j, :, cols]
            for d in range(1, SHORT):
                total = total + short_ref[j, d : d + 1, cols] * ext[j, TILE - d : 2 * TILE - d]
            feats.append(total.astype(BF16).astype(F32))
        product = (feats[1] * feats[2]).astype(BF16).astype(F32)
        first_ref[0, :, cols] = feats[0]
        first_ref[1, :, cols] = product
        decay = decay_ref[:, cols]
        own = modal_sums([product], decay, row_iota())
        whole = sums_ref[0, :, cols] + own * jnp.exp(-float(row_count - TILE) * decay)
        part = sums_ref[1, :, cols] + own * jnp.exp(-float(row_count - MED - TILE) * decay)
        part_ref[:, cols] = part.astype(BF16)
        whole = whole.astype(BF16)
        for i in range(spread_ref.shape[0]):
            spread_ref[i, :, cols] = whole
        return 0

    lax.fori_loop(0, part_ref.shape[1] // LANES, group_body, 0)


def direct_kernel(g_ref, edge_ref, p_ref, first_ref, decay_ref, near_ref, sums_ref, shifted, signal):
    row_count = p_ref.shape[0]
    out_tiles = row_count // TILE
    lead_tiles = MED // TILE
    block_tiles = BLOCK // TILE
    reach = g_ref.shape[0]

    def group_body(group, _):
        cols = lanes_of(group)
        for s in range(TILE):
            shifted[s, 0:TILE] = jnp.zeros((TILE, LANES), F32)
            shifted[s, s : s + reach] = g_ref[:, cols]
        lead = edge_ref[3 * EDGE : 3 * EDGE + MED, cols].astype(F32)
        signal[0:MED] = lead
        signal[MED : MED + row_count] = p_ref[:, cols].astype(F32)
        signal[MED : MED + TILE] = first_ref[1, :, cols]
        for b in range(sums_ref.shape[0]):
            tiles = tiles_of(lead[BLOCK * b : BLOCK * (b + 1)])
            sums_ref[b, :, cols] = modal_sums(tiles, decay_ref[:, cols], row_iota())

        def shift_body(s, acc):
            acc = list(acc)
            for j in range(lead_tiles + out_tiles):
                row = jnp.broadcast_to(signal[pl.ds(TILE * j + s, 1), :], (TILE, LANES))
                for i in range(max(0, j - lead_tiles), min(out_tiles, (j // block_tiles + 1) * block_tiles)):
                    off = TILE * (i + lead_tiles - j)
                    acc[i] = acc[i] + row * shifted[s, off : off + TILE]
            return tuple(acc)

        acc = lax.fori_loop(0, TILE, shift_body, tuple(jnp.zeros((TILE, LANES), F32) for _ in range(out_tiles)))
        near_ref[:, cols] = jnp.concatenate(acc, 0)
        return 0

    lax.fori_loop(0, p_ref.shape[1] // LANES, group_body, 0)


def combine_kernel(index_ref, wm_ref, decay_ref, states_ref, part_ref, lead_ref, near_ref, q_ref, first_ref, gain_ref,
                   gated_ref, sums_ref, entry, squares):
    row_count = q_ref.shape[0]
    block_tiles = BLOCK // TILE
    squares[...] = jnp.zeros(squares.shape, F32)
    span = jnp.exp(-float(row_count) * decay_ref[...])
    block_span = jnp.exp(-float(BLOCK) * decay_ref[...])

    def carry_body(j, carried):
        return carried * span + states_ref[j].astype(F32)

    carried = lax.fori_loop(0, index_ref[0] - 1, carry_body, jnp.zeros(span.shape, F32))
    state = part_ref[...].astype(F32) + jnp.exp(-float(row_count - MED) * decay_ref[...]) * carried
    for b in range(entry.shape[0]):
        entry[b] = state * wm_ref[...]
        if b < lead_ref.shape[0]:
            state = state * block_span + lead_ref[b]

    def group_body(group, _):
        cols = lanes_of(group)
        rows = row_iota()
        decay = decay_ref[:, cols]
        eight = jnp.exp(-TILE * decay)
        acc = tiles_of(near_ref[:, cols])
        for n in range(MODES):
            step = jnp.broadcast_to(eight[n : n + 1], (TILE, LANES))
            powers = jnp.exp(-decay[n : n + 1] * (rows + 2))
            terms = [entry[b, n : n + 1, cols] * powers for b in range(entry.shape[0])]
            for i in range(block_tiles):
                for b in range(entry.shape[0]):
                    acc[b * block_tiles + i] = acc[b * block_tiles + i] + terms[b]
                    if i < block_tiles - 1:
                        terms[b] = terms[b] * step
        query = q_ref[:, cols].astype(F32)
        gated = jnp.concatenate(acc, 0) * jnp.concatenate([first_ref[0, :, cols], query[TILE:]], 0)
        gated_ref[:, cols] = gated * gain_ref[:, cols]
        squares[...] = squares[...] + gated * gated
        return 0

    lax.fori_loop(0, q_ref.shape[1] // LANES, group_body, 0)
    sums = lax.dot_general(
        jnp.ones((TILE, LANES), F32), squares[...], (((1,), (1,)), ((), ())),
        precision=lax.Precision.HIGHEST, preferred_element_type=F32,
    )
    for i in range(sums_ref.shape[0]):
        sums_ref[i] = sums


def norm_kernel(gated_ref, sums_ref, out_ref):
    total = sums_ref[0]
    for i in range(1, sums_ref.shape[0]):
        total = total + sums_ref[i]
    scale = jnp.transpose(lax.rsqrt(total / C + EPS))[:, 0:1]
    out_ref[...] = (gated_ref[...] * scale).astype(BF16)


def shape(dims, dtype):
    return jax.ShapeDtypeStruct(dims, dtype)


def from_behind(block, axis):
    return lax.ppermute(block, axis, [(i - 1, i) for i in range(1, lax.axis_size(axis))])


def shape(dims, dtype=F32):
    return jax.ShapeDtypeStruct(dims, dtype)


def call(kernel, name, out_shape, scratch, args, scalars=0):
    vmem, smem = (pl.BlockSpec(memory_space=space) for space in (pltpu.VMEM, pltpu.SMEM))
    return pl.pallas_call(
        kernel,
        out_shape=out_shape,
        in_specs=[smem] * scalars + [vmem] * (len(args) - scalars),
        out_specs=jax.tree.map(lambda _: vmem, out_shape),
        scratch_shapes=[pltpu.VMEM(dims, F32) for dims in scratch],
        compiler_params=PARAMS,
        name=name,
    )(*args)


def from_behind(block, axis):
    return lax.ppermute(block, axis, [(i - 1, i) for i in range(1, lax.axis_size(axis))])


def on_device(projected, short_filter, medium_filter, decay, residues, skip_gain, out_gain):
    _, rows, chans = projected.shape
    ctx, ch = lax.axis_size("ctx"), lax.axis_size("ch")
    reach = MED + BLOCK
    short = jnp.transpose(short_filter, (1, 0, 2))
    params = (medium_filter, decay, residues, skip_gain[None], out_gain[None])
    queries, product, edge, head, *params = call(
        feature_kernel,
        "features",
        (
            shape((rows, chans), BF16),
            shape((rows, chans), BF16),
            shape((3 * EDGE + MED, chans), BF16),
            shape((3, TILE, chans)),
        )
        + tuple(shape(p.shape, p.dtype) for p in params),
        [(3, rows + TILE, LANES)],
        (projected, short) + params,
    )
    medium_filter, decay, residues, skip_gain, out_gain = params
    edge = from_behind(edge, "ctx")
    taps, reach_weights, partial = call(
        table_kernel,
        "tables",
        (shape((reach, chans)), shape((MODES, chans)), shape((2, MODES, chans))),
        [(MED, LANES), (TILE, MED + TILE, LANES)],
        (product, medium_filter, decay, residues, skip_gain),
    )
    spread, part, first = call(
        functools.partial(first_kernel, row_count=rows),
        "first",
        (shape((ctx, MODES, chans), BF16), shape((MODES, chans), BF16), shape((2, TILE, chans))),
        [(3, 2 * TILE, LANES)],
        (edge, head, short, decay, partial),
    )
    states = lax.all_to_all(spread, "ctx", 0, 0, tiled=True)
    part = from_behind(part, "ctx")
    near, lead = call(
        direct_kernel,
        "direct",
        (shape((rows, chans)), shape((MED // BLOCK, MODES, chans))),
        [(TILE, reach + TILE, LANES), (MED + rows, LANES)],
        (taps, edge, product, first, decay),
    )
    gated, sums = call(
        combine_kernel,
        "combine",
        (shape((rows, chans)), shape((ch, TILE, rows))),
        [(rows // BLOCK, MODES, chans), (rows, LANES)],
        (lax.axis_index("ctx").reshape(1), reach_weights, decay, states, part, lead, near, queries, first, out_gain),
        scalars=1,
    )
    sums = lax.all_to_all(sums, "ch", 0, 0, tiled=True)
    return pl.pallas_call(
        norm_kernel, out_shape=shape((rows, chans), BF16), compiler_params=PARAMS, name="norm"
    )(gated, sums)


def solution(mesh):
    in_specs = (
        P(None, "ctx", "ch"),
        P(None, None, "ch"),
        P(None, "ch"),
        P(None, "ch"),
        P(None, "ch"),
        P("ch"),
        P("ch"),
    )
    return jax.shard_map(on_device, mesh=mesh, in_specs=in_specs, out_specs=P("ctx", "ch"), check_vma=False)
```

time: 56 us -> 51.5 us (0.920)
  the two profiles are of different devices: /device:TPU:2 before, /device:TPU:1 now
where the time goes in v3:
time: 51.5 us; the launch traced here: 50.9 us
  starting transfers between devices  16 us (31%)
  blocking collectives  15.3 us (30%)
  Pallas kernels  11.6 us (23%)
  local copies, waits for them, and re-layouts  4.98 us (10%)
  waiting for transfers between devices  2.95 us (6%)
    all_to_all x1, blocking collectives, on_device(): sums = lax.all_to_all(sums, 'ch', 0, 0, tiled=True)  15.3 us
    pallas_call x5, Pallas kernels, call(): pl.pallas_call(kernel, out_shape=out_shape, in_specs=[smem] * scalars + [...  10.7 us
    ppermute x2, starting transfers between devices, from_behind(): lax.ppermute(block, axis, [(i - 1, i) for i in range(1, lax.axis_size(axi...  8.13 us
    all_to_all x1, starting transfers between devices, on_device(): states = lax.all_to_all(spread, 'ctx', 0, 0, tiled=True)  7.83 us
    unnamed x16, local copies, waits for them, and re-layouts  4.98 us
    all_to_all x1, waiting for transfers between devices, on_device(): states = lax.all_to_all(spread, 'ctx', 0, 0, tiled=True)  2.94 us
  transfers between devices with their start and end apart: 3, of which 1 were waited for; matrix products, arithmetic and copies ran while one was open for 0% of the time, Pallas kernels for 16%

profile of v3, /device:TPU:1, one launch (start us, length us, event | category | flops | bytes accessed | tf_op | source)
XLA Modules:
  0.0 50.9 jit_solution(7826821461282868259)
XLA Ops:
  0.0 0.0 copy-start.7
  0.0 0.0 copy-start.6
  0.0 0.7 %copy-done.7 = f32[512]{0:T(512)S(1)} copy-done((f32[512]{0:T(512)S(1)}, f32[512]{0:T(512)}, u32[]{:S(2)}) %copy-start.7) | copy-done | bytes 2072
  0.7 0.0 copy-done.6
  0.7 0.0 copy-start
  0.7 1.1 %copy-done = bf16[3,192,512]{2,1,0:T(8,128)(2,1)S(1)} copy-done((bf16[3,192,512]{2,1,0:T(8,128)(2,1)S(1)}, bf16[3,192,512]{2,1,0:T(8,128)(2,1)}, u32[]{:S(2)}) %copy-start) | copy-done | bytes 589848
  1.8 0.0 copy-start.1
  1.8 0.8 %copy-done.1 = f32[7,3,512]{2,0,1:T(8,128)S(1)} copy-done((f32[7,3,512]{2,0,1:T(8,128)S(1)}, f32[7,3,512]{2,0,1:T(8,128)}, u32[]{:S(2)}) %copy-start.1) | copy-done | bytes 43032
  2.6 0.0 copy-start.3
  2.6 0.9 %copy-done.3 = bf16[128,512]{1,0:T(8,128)(2,1)S(1)} copy-done((bf16[128,512]{1,0:T(8,128)(2,1)S(1)}, bf16[128,512]{1,0:T(8,128)(2,1)}, u32[]{:S(2)}) %copy-start.3) | copy-done | bytes 131096
  3.5 0.0 copy-start.4
  3.5 0.8 %copy-done.4 = f32[16,512]{1,0:T(8,128)S(1)} copy-done((f32[16,512]{1,0:T(8,128)S(1)}, f32[16,512]{1,0:T(8,128)}, u32[]{:S(2)}) %copy-start.4) | copy-done | bytes 32792
  4.2 0.0 copy-start.5
  4.2 0.8 %copy-done.5 = f32[16,512]{1,0:T(8,128)S(1)} copy-done((f32[16,512]{1,0:T(8,128)S(1)}, f32[16,512]{1,0:T(8,128)}, u32[]{:S(2)}) %copy-start.5) | copy-done | bytes 32792
  5.0 0.8 %features.1 = (bf16[192,512]{1,0:T(8,128)(2,1)S(1)}, bf16[192,512]{1,0:T(8,128)(2,1)S(1)}, bf16[176,512]{1,0:T(8,128)(2,1)S(1)}, f32[3,8,512]{2,1,0:T(8,128)S(1)...) custom-call(bf16[3,192,512]{2,1,0:T(8,128)(2,1)S(1)} %copy-done, ...), custom_call_target="tpu_custom_call" | custom-call | tf_op jit(solution)/shard_map/features/pallas_call | solution.py:275
  5.7 4.6 %collective-permute-start = (bf16[176,512]{1,0:T(8,128)(2,1)S(1)}, bf16[176,512]{1,0:T(8,128)(2,1)S(1)}, u32[]{:S(2)}, u32[]{:S(2)}) collective-permute-start(bf16[176,512]{1,0:T(8,128)(2,1)S(1)} %get-tuple-element.30), channel_id=1, source_target_pairs={{0,8},{8,16},{16,24},{24,32},{32,40},{40,48},{48,56},{56,64},{64,7... | collective-permute-start | bytes 540680 | tf_op jit(solution)/shard_map/ppermute | solution.py:287
  10.3 0.0 copy-start.2
  10.4 2.9 %tables.1 = (f32[192,512]{1,0:T(8,128)S(1)}, f32[16,512]{1,0:T(8,128)S(1)}, f32[2,16,512]{2,1,0:T(8,128)S(1)}) custom-call(bf16[192,512]{1,0:T(8,128)(2,1)S(1)} %get-tuple-element.24.p_ref, bf16[128,512]{1,0:T(8,128)(2,1)S(1)} %get-tuple-element.25.med_ref, f32[16,512]{1,0:T(8,128)S(1)} %get-tuple-element.26.decay_ref, ...), custom_call_target="tpu_custom_call" | custom-call | tf_op jit(solution)/shard_map/tables/pallas_call | solution.py:275
  13.3 0.0 collective-permute-done.edge_ref
  13.3 0.0 copy-done.2
  13.3 1.1 %first.1 = (bf16[32,16,512]{2,1,0:T(8,128)(2,1)}, bf16[16,512]{1,0:T(8,128)(2,1)S(1)}, f32[2,8,512]{2,1,0:T(8,128)S(1)}) custom-call(bf16[176,512]{1,0:T(8,128)(2,1)S(1)} %collective-permute-done.edge_ref, f32[3,8,512]{2,1,0:T(8,128)S(1)} %get-tuple-element.31.head_ref, f32[3,7,512]{2,1,0:T(8,128)S(1)} %bitcast.5, ...), custom_call_target="tpu_custom_call" | custom-call | tf_op jit(solution)/shard_map/first/pallas_call | solution.py:275
  14.4 7.8 %all-to-all-start = ((bf16[32,16,512]{2,1,0:T(8,128)(2,1)}), bf16[32,16,512]{2,1,0:T(8,128)(2,1)S(1)}, u32[]{:S(2)}, u32[]{:S(2)}) async-start(bf16[32,16,512]{2,1,0:T(8,128)(2,1)} %get-tuple-element.33), calls=%async_computation | async-start | bytes 1048576 | tf_op jit(solution)/shard_map/all_to_all | solution.py:325
  22.3 3.5 %collective-permute-start.1 = (bf16[16,512]{1,0:T(8,128)(2,1)S(1)}, bf16[16,512]{1,0:T(8,128)(2,1)S(1)}, u32[]{:S(2)}, u32[]{:S(2)}) collective-permute-start(bf16[16,512]{1,0:T(8,128)(2,1)S(1)} %get-tuple-element.34), channel_id=1, source_target_pairs={{0,8},{8,16},{16,24},{24,32},{32,40},{40,48},{48,56},{56,64},{64,7... | collective-permute-start | bytes 49160 | tf_op jit(solution)/shard_map/ppermute | solution.py:287
  25.8 5.1 %direct.1 = (f32[192,512]{1,0:T(8,128)S(1)}, f32[2,16,512]{2,1,0:T(8,128)S(1)}) custom-call(f32[192,512]{1,0:T(8,128)S(1)} %get-tuple-element.35.g_ref, bf16[176,512]{1,0:T(8,128)(2,1)S(1)} %collective-permute-done.edge_ref, bf16[192,512]{1,0:T(8,128)(2,1)S(1)} %get-tuple-element.24.p_ref, f32[2,8,512]{2,1,0:T(8,128)S(1)} %get-tuple-element.36.first_ref, ...), custom_call_target="tpu_custom_call" | custom-call | tf_op jit(solution)/shard_map/direct/pallas_call | solution.py:275
  30.9 0.0 collective-permute-done.1.part_ref
  30.9 2.9 %all-to-all-done.states_ref = bf16[32,16,512]{2,1,0:T(8,128)(2,1)S(1)} async-done(((bf16[32,16,512]{2,1,0:T(8,128)(2,1)}), bf16[32,16,512]{2,1,0:T(8,128)(2,1)S(1)}, u32[]{:S(2)}, u32[]{:S(2)}) %all-to-all-start) | async-done | bytes 524320 | tf_op jit(solution)/shard_map/all_to_all | solution.py:325
  33.9 0.8 %combine.1 = (f32[192,512]{1,0:T(8,128)S(1)}, f32[8,8,192]{2,1,0:T(8,128)S(1)}) custom-call(s32[1]{0:T(128)} %bitcast.index_ref, f32[16,512]{1,0:T(8,128)S(1)} %get-tuple-element.29.wm_ref, f32[16,512]{1,0:T(8,128)S(1)} %get-tuple-element.26.decay_ref, bf16[32,16,512]{2,1,0:T(8,128)(2,1)S(1)} %all-to-all-done.states_ref, ...), custom_call_target="tpu_custom_call" | custom-call | tf_op jit(solution)/shard_map/combine/pallas_call | solution.py:275
  34.7 15.3 %all_to_all.10.sums_ref = f32[8,8,192]{2,1,0:T(8,128)S(1)} all-to-all(f32[8,8,192]{2,1,0:T(8,128)S(1)} %get-tuple-element.42), channel_id=1, replica_groups=mesh['ctx'=32,'ch'=8] {'ch'}, dimensions={0} | all-to-all | bytes 98304 | tf_op jit(solution)/shard_map/all_to_all | solution.py:342
  50.0 0.9 %norm.1 = bf16[192,512]{1,0:T(8,128)(2,1)} custom-call(f32[192,512]{1,0:T(8,128)S(1)} %get-tuple-element.41.gated_ref, f32[8,8,192]{2,1,0:T(8,128)S(1)} %all_to_all.10.sums_ref), custom_call_target="tpu_custom_call" | custom-call | tf_op jit(solution)/shard_map/norm/pallas_call | solution.py:343
Async XLA Ops:
  0.0 0.7 %copy-start.7 = (f32[512]{0:T(512)S(1)}, f32[512]{0:T(512)}, u32[]{:S(2)}) copy-start(f32[512]{0:T(512)} %param.13) | copy-start | bytes 6148
  0.0 0.7 %copy-start.6 = (f32[512]{0:T(512)S(1)}, f32[512]{0:T(512)}, u32[]{:S(2)}) copy-start(f32[512]{0:T(512)} %param.12) | copy-start | bytes 6148
  0.7 1.1 %copy-start = (bf16[3,192,512]{2,1,0:T(8,128)(2,1)S(1)}, bf16[3,192,512]{2,1,0:T(8,128)(2,1)}, u32[]{:S(2)}) copy-start(bf16[3,192,512]{2,1,0:T(8,128)(2,1)} %proj_ref.1) | copy-start | bytes 1769476
  1.8 0.8 %copy-start.1 = (f32[7,3,512]{2,0,1:T(8,128)S(1)}, f32[7,3,512]{2,0,1:T(8,128)}, u32[]{:S(2)}) copy-start(f32[7,3,512]{2,0,1:T(8,128)} %param.8) | copy-start | bytes 129028
  2.6 0.9 %copy-start.3 = (bf16[128,512]{1,0:T(8,128)(2,1)S(1)}, bf16[128,512]{1,0:T(8,128)(2,1)}, u32[]{:S(2)}) copy-start(bf16[128,512]{1,0:T(8,128)(2,1)} %refs_0_.1) | copy-start | bytes 393220
  3.5 0.8 %copy-start.4 = (f32[16,512]{1,0:T(8,128)S(1)}, f32[16,512]{1,0:T(8,128)}, u32[]{:S(2)}) copy-start(f32[16,512]{1,0:T(8,128)} %refs_1_.1) | copy-start | bytes 98308
  4.2 0.8 %copy-start.5 = (f32[16,512]{1,0:T(8,128)S(1)}, f32[16,512]{1,0:T(8,128)}, u32[]{:S(2)}) copy-start(f32[16,512]{1,0:T(8,128)} %refs_2_.1) | copy-start | bytes 98308
  5.7 7.6 %collective-permute-start = (bf16[176,512]{1,0:T(8,128)(2,1)S(1)}, bf16[176,512]{1,0:T(8,128)(2,1)S(1)}, u32[]{:S(2)}, u32[]{:S(2)}) collective-permute-start(bf16[176,512]{1,0:T(8,128)(2,1)S(1)} %get-tuple-element.30), channel_id=1, source_target_pairs={{0,8},{8,16},{16,24},{24,32},{32,40},{40,48},{48,56},{56,64},{64,7... | collective-permute-start | bytes 540680 | tf_op jit(solution)/shard_map/ppermute | solution.py:287
  10.3 3.0 %copy-start.2 = (f32[7,3,512]{2,0,1:T(8,128)S(1)}, f32[7,3,512]{2,0,1:T(8,128)}, u32[]{:S(2)}) copy-start(f32[7,3,512]{2,0,1:T(8,128)} %param.8) | copy-start | bytes 129028
  14.4 19.5 %all-to-all-start = ((bf16[32,16,512]{2,1,0:T(8,128)(2,1)}), bf16[32,16,512]{2,1,0:T(8,128)(2,1)S(1)}, u32[]{:S(2)}, u32[]{:S(2)}) async-start(bf16[32,16,512]{2,1,0:T(8,128)(2,1)} %get-tuple-element.33), calls=%async_computation | async-start | bytes 1048576 | tf_op jit(solution)/shard_map/all_to_all | solution.py:325
  22.3 8.7 %collective-permute-start.1 = (bf16[16,512]{1,0:T(8,128)(2,1)S(1)}, bf16[16,512]{1,0:T(8,128)(2,1)S(1)}, u32[]{:S(2)}, u32[]{:S(2)}) collective-permute-start(bf16[16,512]{1,0:T(8,128)(2,1)S(1)} %get-tuple-element.34), channel_id=1, source_target_pairs={{0,8},{8,16},{16,24},{24,32},{32,40},{40,48},{48,56},{56,64},{64,7... | collective-permute-start | bytes 49160 | tf_op jit(solution)/shard_map/ppermute | solution.py:287

commit v4 on v3

v4 whole, which is shorter than its diff:
```python
import jax
import jax.numpy as jnp
from jax import lax
from jax.experimental import pallas as pl
from jax.experimental.pallas import tpu as pltpu
from jax.sharding import PartitionSpec as P

C = 4096
SHORT = 7
MED = 128
MODES = 16
EPS = 1e-06
LANES = 128
TILE = 8
EDGE = 16
BLOCK = 64
F32 = jnp.float32
BF16 = jnp.bfloat16
PARAMS = pltpu.CompilerParams(vmem_limit_bytes=48 * 1024 * 1024)


def row_iota():
    return lax.broadcasted_iota(jnp.int32, (TILE, LANES), 0).astype(F32)


def lanes_of(group):
    return pl.ds(pl.multiple_of(group * LANES, LANES), LANES)


def one_minus_exp(x):
    return x * (1 - x * (1 / 2) * (1 - x * (1 / 3) * (1 - x * (1 / 4) * (1 - x * (1 / 5) * (1 - x * (1 / 6))))))


def tiles_of(array):
    return [array[TILE * i : TILE * (i + 1)] for i in range(array.shape[0] // TILE)]


def modal_sums(tiles, decay, rows):
    eight = jnp.exp(-TILE * decay)
    sums = []
    for n in range(MODES):
        step = jnp.broadcast_to(eight[n : n + 1], (TILE, LANES))
        state = tiles[0]
        for tile in tiles[1:]:
            state = state * step + tile
        sums.append(jnp.sum(state * jnp.exp(-decay[n : n + 1] * (TILE - 1 - rows)), axis=0, keepdims=True))
    return jnp.concatenate(sums, 0)


def edge_kernel(proj_ref, edge_ref, raw_ref):
    rows = proj_ref.shape[1]
    edge_ref[...] = proj_ref[1:, rows - EDGE :]
    raw_ref[...] = proj_ref[...]


def short_sum(ext, taps, start, rows, first=0):
    total = 0.0
    for d in range(first, SHORT):
        total = total + taps[d : d + 1] * ext[start - d : start - d + rows]
    return total


def feature_kernel(raw_ref, short_ref, p_ref, tail_ref, head_ref, ext):
    row_count = raw_ref.shape[1]

    def group_body(group, _):
        cols = lanes_of(group)
        feats = []
        for j in range(2):
            ext[j, 0:TILE] = jnp.zeros((TILE, LANES), F32)
            ext[j, TILE:] = raw_ref[1 + j, :, cols].astype(F32)
            total = short_sum(ext.at[j], short_ref[1 + j, :, cols], TILE, row_count)
            head_ref[j, :, cols] = total[0:TILE]
            feats.append(total.astype(BF16).astype(F32))
        product = (feats[0] * feats[1]).astype(BF16)
        p_ref[:, cols] = product
        tail_ref[0:MED, cols] = product[row_count - MED :]
        tail_ref[MED:, cols] = raw_ref[0, row_count - EDGE :, cols]
        return 0

    lax.fori_loop(0, p_ref.shape[1] // LANES, group_body, 0)


def first_kernel(index_ref, halo_ref, head_ref, short_ref, decay_ref, p_ref, spread_ref, first_ref, ext):
    following = jnp.minimum(index_ref[0] + 1, spread_ref.shape[0] - 1)
    part_tiles = (p_ref.shape[0] - MED) // TILE

    def group_body(group, _):
        cols = lanes_of(group)
        feats = []
        for j in range(2):
            ext[group, j, 0:TILE] = halo_ref[j, :, cols].astype(F32)[EDGE - TILE :]
            ext[group, j, TILE:] = jnp.zeros((TILE, LANES), F32)
            total = head_ref[j, :, cols] + short_sum(ext.at[group, j], short_ref[1 + j, :, cols], TILE, TILE, 1)
            feats.append(total.astype(BF16).astype(F32))
        product = (feats[0] * feats[1]).astype(BF16).astype(F32)
        first_ref[:, cols] = product
        tiles = tiles_of(p_ref[:, cols].astype(F32))
        decay = decay_ref[:, cols]
        eight = jnp.exp(-TILE * decay)
        wholes, parts = [], []
        for n in range(MODES):
            step = jnp.broadcast_to(eight[n : n + 1], (TILE, LANES))
            close = jnp.exp(-decay[n : n + 1] * (TILE - 1 - row_iota()))
            state = product
            for i in range(1, len(tiles)):
                if i == part_tiles:
                    parts.append(jnp.sum(state * close, axis=0, keepdims=True))
                state = state * step + tiles[i]
            wholes.append(jnp.sum(state * close, axis=0, keepdims=True))
        whole = jnp.concatenate(wholes, 0).astype(BF16)
        for i in range(spread_ref.shape[0]):
            spread_ref[i, :, cols] = whole
        spread_ref[following, :, cols] = jnp.concatenate(parts, 0).astype(BF16)
        return 0

    lax.fori_loop(0, spread_ref.shape[2] // LANES, group_body, 0, unroll=True)


def row_of(ref, row):
    return jnp.broadcast_to(ref[pl.ds(row, 1), :], (TILE, LANES))


def tile_at(bank, index):
    return bank[TILE * index : TILE * (index + 1)]


def pair_up(signal, pairs):
    half = BLOCK // 2
    for b in range(signal.shape[0] // BLOCK):
        pairs[half * b : half * (b + 1)] = signal[BLOCK * b : BLOCK * b + half] + signal[BLOCK * b + half : BLOCK * (b + 1)]


def no_sums(tiles):
    return tuple(jnp.zeros((TILE, LANES), F32) for _ in range(tiles + tiles // 2))


def with_pairs(acc, tiles):
    half = BLOCK // TILE // 2
    return [acc[i] + acc[tiles + i // (2 * half) * half + i % half] for i in range(tiles)]


def add_block(acc, tiles, out, block, distance, bank, signal, pairs, s):
    full = BLOCK // TILE
    half = full // 2
    base = full * distance
    reach = range(1 - half, half)
    mid = {o: tile_at(bank, base + o) for o in reach}
    upper = {o: tile_at(bank, base + o - half) - mid[o] for o in reach}
    lower = {o: tile_at(bank, base + o + half) - mid[o] for o in reach}
    for j in range(half):
        late = row_of(signal, TILE * (full * block + half + j) + s)
        early = row_of(signal, TILE * (full * block + j) + s)
        both = row_of(pairs, TILE * (half * block + j) + s)
        for i in range(half):
            at = full * out + i
            acc[at] = acc[at] + late * upper[i - j]
            acc[at + half] = acc[at + half] + early * lower[i - j]
            acc[tiles + half * out + i] = acc[tiles + half * out + i] + both * mid[i - j]


def direct_kernel(med_ref, decay_ref, res_ref, skip_ref, gain_ref, short_ref, tail_ref, raw_ref, p_ref, first_ref,
                  q_ref, wm_ref, near_ref, sums_ref, held_ref, med_f32, shifted, signal, pairs, ext):
    row_count = p_ref.shape[0]
    out_tiles = row_count // TILE
    block_tiles = BLOCK // TILE
    blocks = sums_ref.shape[0]
    med_tiles = MED // TILE
    far_tiles = BLOCK // TILE
    reach = MED + BLOCK
    held_ref[...] = gain_ref[...]

    def group_body(group, _):
        cols = lanes_of(group)
        rows = row_iota()
        decay = decay_ref[:, cols]
        weights = res_ref[:, cols] * jnp.sqrt(one_minus_exp(2.0 * decay))
        eight = jnp.exp(-TILE * decay)
        med = med_ref[:, cols].astype(F32)
        med_f32[...] = med
        near = [jnp.zeros((TILE, LANES), F32) for _ in range(med_tiles)]
        far = [jnp.zeros((TILE, LANES), F32) for _ in range(far_tiles)]
        for n in range(MODES):
            rate = decay[n : n + 1]
            step = jnp.broadcast_to(eight[n : n + 1], (TILE, LANES))
            weight = weights[n : n + 1]
            term = weight * jnp.exp(-rate * rows)
            state = jnp.zeros((TILE, LANES), F32)
            for i in range(med_tiles):
                near[i] = near[i] + term
                term = term * step
                state = state * step + med[TILE * i : TILE * (i + 1)]
            reach_weight = jnp.sum(state * jnp.exp(-rate * (TILE - 1 - rows)), axis=0, keepdims=True) * weight
            wm_ref[n : n + 1, cols] = reach_weight
            term = reach_weight * jnp.exp(-rate * (rows + 1))
            for i in range(far_tiles):
                far[i] = far[i] + term
                term = term * step
        near[0] = near[0] + jnp.where(rows == 0, skip_ref[:, cols], 0.0)
        taps = jnp.concatenate(near, 0)
        for s in range(TILE):
            shifted[s, 0:TILE] = jnp.zeros((TILE, LANES), F32)
            shifted[s, s : s + MED] = taps

        def taps_body(s, acc):
            acc = list(acc)
            bank = [shifted[s, TILE * i : TILE * (i + 1)] for i in range(med_tiles)]
            for j in range(med_tiles):
                row = jnp.broadcast_to(med_f32[pl.ds(TILE * j + s, 1), :], (TILE, LANES))
                for i in range(j, med_tiles):
                    acc[i] = acc[i] + row * bank[i - j]
            return tuple(acc)

        acc = lax.fori_loop(0, TILE, taps_body, tuple(jnp.zeros((TILE, LANES), F32) for _ in range(med_tiles)))
        taps = jnp.concatenate(list(acc) + far, 0)
        for s in range(TILE):
            shifted[s, 0:TILE] = jnp.zeros((TILE, LANES), F32)
            shifted[s, s : s + reach] = taps
        tail = tail_ref[:, cols].astype(F32)
        lead = tail[0:MED]
        ext[0:TILE] = tail[MED + EDGE - TILE :]
        ext[TILE:] = raw_ref[0, :, cols].astype(F32)
        q_ref[:, cols] = short_sum(ext, short_ref[0, :, cols], TILE, row_count).astype(BF16)
        signal[0:MED] = lead
        signal[MED : MED + row_count] = p_ref[:, cols].astype(F32)
        signal[MED : MED + TILE] = first_ref[:, cols]
        for b in range(blocks):
            tiles = tiles_of(lead[BLOCK * b : BLOCK * (b + 1)])
            sums_ref[b, :, cols] = modal_sums(tiles, decay, rows)

        pair_up(signal, pairs)

        def direct_body(s, acc):
            bank = shifted.at[s]
            acc = list(acc)
            for j in range(out_tiles):
                row = row_of(signal, MED + TILE * j + s)
                for i in range(j, (j // block_tiles + 1) * block_tiles):
                    acc[i] = acc[i] + row * tile_at(bank, i - j)
            for out in range(out_tiles // block_tiles):
                for distance in range(1, blocks + 1):
                    add_block(acc, out_tiles, out, out + blocks - distance, distance, bank, signal, pairs, s)
            return tuple(acc)

        acc = lax.fori_loop(0, TILE, direct_body, no_sums(out_tiles))
        near_ref[:, cols] = jnp.concatenate(with_pairs(acc, out_tiles), 0)
        return 0

    lax.fori_loop(0, p_ref.shape[1] // LANES, group_body, 0)


def combine_kernel(index_ref, wm_ref, decay_ref, states_ref, lead_ref, near_ref, q_ref, gain_ref,
                   gated_ref, sums_ref, entry, squares):
    row_count = q_ref.shape[0]
    block_tiles = BLOCK // TILE
    own = index_ref[0]
    squares[...] = jnp.zeros(squares.shape, F32)
    span = jnp.exp(-float(row_count) * decay_ref[...])
    block_span = jnp.exp(-float(BLOCK) * decay_ref[...])

    def carry_body(j, carried):
        return carried * span + states_ref[j].astype(F32)

    carried = lax.fori_loop(0, own - 1, carry_body, jnp.zeros(span.shape, F32))
    part = states_ref[jnp.maximum(own - 1, 0)].astype(F32)
    state = jnp.where(own > 0, part, 0.0) + jnp.exp(-float(row_count - MED) * decay_ref[...]) * carried
    for b in range(entry.shape[0]):
        entry[b] = state * wm_ref[...]
        if b < lead_ref.shape[0]:
            state = state * block_span + lead_ref[b]

    def group_body(group, _):
        cols = lanes_of(group)
        rows = row_iota()
        decay = decay_ref[:, cols]
        eight = jnp.exp(-TILE * decay)
        acc = tiles_of(near_ref[:, cols])
        for n in range(MODES):
            step = jnp.broadcast_to(eight[n : n + 1], (TILE, LANES))
            powers = jnp.exp(-decay[n : n + 1] * (rows + 2))
            terms = [entry[b, n : n + 1, cols] * powers for b in range(entry.shape[0])]
            for i in range(block_tiles):
                for b in range(entry.shape[0]):
                    acc[b * block_tiles + i] = acc[b * block_tiles + i] + terms[b]
                    if i < block_tiles - 1:
                        terms[b] = terms[b] * step
        gated = jnp.concatenate(acc, 0) * q_ref[:, cols].astype(F32)
        gated_ref[:, cols] = gated * gain_ref[:, cols]
        squares[...] = squares[...] + gated * gated
        return 0

    lax.fori_loop(0, q_ref.shape[1] // LANES, group_body, 0)
    sums = lax.dot_general(
        jnp.ones((TILE, LANES), F32), squares[...], (((1,), (1,)), ((), ())),
        precision=lax.Precision.HIGHEST, preferred_element_type=F32,
    )
    for i in range(sums_ref.shape[0]):
        sums_ref[i] = sums[0:1]


def norm_kernel(gated_ref, sums_ref, out_ref):
    total = sums_ref[0]
    for i in range(1, sums_ref.shape[0]):
        total = total + sums_ref[i]
    scale = jnp.broadcast_to(lax.rsqrt(total / C + EPS), (TILE, total.shape[1]))
    scale = jnp.transpose(scale)[:, 0:1]
    out_ref[...] = (gated_ref[...] * scale).astype(BF16)


def shape(dims, dtype):
    return jax.ShapeDtypeStruct(dims, dtype)


def cost(flops):
    return pl.CostEstimate(flops=int(flops), bytes_accessed=0, transcendentals=0)


def from_behind(block, axis):
    return lax.ppermute(block, axis, [(i - 1, i) for i in range(1, lax.axis_size(axis))])


def shape(dims, dtype=F32):
    return jax.ShapeDtypeStruct(dims, dtype)


def call(kernel, name, out_shape, scratch, args, scalars=0, cost=None):
    vmem, smem = (pl.BlockSpec(memory_space=space) for space in (pltpu.VMEM, pltpu.SMEM))
    return pl.pallas_call(
        kernel,
        out_shape=out_shape,
        in_specs=[smem] * scalars + [vmem] * (len(args) - scalars),
        out_specs=jax.tree.map(lambda _: vmem, out_shape),
        scratch_shapes=[pltpu.VMEM(dims, F32) for dims in scratch],
        compiler_params=PARAMS,
        cost_estimate=cost,
        name=name,
    )(*args)


def cost(flops):
    return pl.CostEstimate(flops=int(flops), bytes_accessed=0, transcendentals=0)


def from_behind(block, axis):
    return lax.ppermute(block, axis, [(i - 1, i) for i in range(1, lax.axis_size(axis))])


def on_device(projected, short_filter, medium_filter, decay, residues, skip_gain, out_gain):
    _, rows, chans = projected.shape
    ctx, ch = lax.axis_size("ctx"), lax.axis_size("ch")
    index = lax.axis_index("ctx").reshape(1)
    short = jnp.pad(jnp.transpose(short_filter, (1, 0, 2)), ((0, 0), (0, TILE - SHORT), (0, 0)))
    edge, raw = call(
        edge_kernel, "edge", (shape((2, EDGE, chans), BF16), shape(projected.shape, BF16)), [], (projected,)
    )
    halo = from_behind(edge, "ctx")
    product, tail, head = call(
        feature_kernel,
        "features",
        (shape((rows, chans), BF16), shape((MED + EDGE, chans), BF16), shape((2, TILE, chans))),
        [(2, rows + TILE, LANES)],
        (raw, short),
        cost=cost(2e9),
    )
    tail = from_behind(tail, "ctx")
    spread, first = call(
        first_kernel,
        "first",
        (shape((ctx, MODES, chans), BF16), shape((TILE, chans))),
        [(chans // LANES, 2, 2 * TILE, LANES)],
        (index, halo, head, short, decay, product),
        scalars=1,
        cost=cost(2e9),
    )
    states = lax.all_to_all(spread, "ctx", 0, 0, tiled=True)
    queries, reach_weights, near, lead, out_gain = call(
        direct_kernel,
        "direct",
        (
            shape((rows, chans), BF16),
            shape((MODES, chans)),
            shape((rows, chans)),
            shape((MED // BLOCK, MODES, chans)),
            shape((1, chans)),
        ),
        [
            (MED, LANES),
            (TILE, MED + BLOCK + TILE, LANES),
            (MED + rows, LANES),
            ((MED + rows) // 2, LANES),
            (rows + TILE, LANES),
        ],
        (medium_filter, decay, residues, skip_gain[None], out_gain[None], short, tail, raw, product, first),
        cost=cost(8e9),
    )
    gated, sums = call(
        combine_kernel,
        "combine",
        (shape((rows, chans)), shape((ch, 1, rows))),
        [(rows // BLOCK, MODES, chans), (rows, LANES)],
        (index, reach_weights, decay, states, lead, near, queries, out_gain),
        scalars=1,
    )
    sums = lax.all_to_all(sums, "ch", 0, 0, tiled=True)
    return pl.pallas_call(
        norm_kernel, out_shape=shape((rows, chans), BF16), compiler_params=PARAMS, name="norm"
    )(gated, sums)


def solution(mesh):
    in_specs = (
        P(None, "ctx", "ch"),
        P(None, None, "ch"),
        P(None, "ch"),
        P(None, "ch"),
        P(None, "ch"),
        P("ch"),
        P("ch"),
    )
    return jax.shard_map(on_device, mesh=mesh, in_specs=in_specs, out_specs=P("ctx", "ch"), check_vma=False)
```

time: 51.5 us -> 45.6 us (0.89)
  local copies, waits for them, and re-layouts: 4.98 us -> 1.74 us
  starting transfers between devices: 16 us -> 13.9 us
  waiting for transfers between devices: 2.95 us -> 3.96 us
  blocking collectives: 15.3 us -> 14.6 us
  Pallas kernels: 11.6 us -> 10.9 us
    unnamed x16 -> x14, local copies, waits for them, and re-layouts: 4.98 us -> 1.73 us
    ppermute x2, starting transfers between devices: 8.13 us -> 6.52 us  [from_behind(): lax.ppermute(block, axis, [(i - 1, i) for i in range(1, lax.axis_size(axi...]
    all_to_all x1, waiting for transfers between devices: 2.94 us -> 3.96 us  [on_device(): states = lax.all_to_all(spread, 'ctx', 0, 0, tiled=True)]
    pallas_call x5, Pallas kernels: 10.7 us -> 9.94 us  [call(): pl.pallas_call(kernel, out_shape=out_shape, in_specs=[smem] * scalars + [...]
    all_to_all x1, blocking collectives: 15.3 us -> 14.6 us  [on_device(): sums = lax.all_to_all(sums, 'ch', 0, 0, tiled=True)]
  transfers between devices with their start and end apart: 3 -> 3, of which waited for: 1 -> 1; matrix products, arithmetic and copies ran while one was open for 0% -> 0% of each run, Pallas kernels for 16% -> 20%
where the time goes in v4:
time: 45.6 us; the launch traced here: 45.2 us
  blocking collectives  14.6 us (32%)
  starting transfers between devices  13.9 us (30%)
  Pallas kernels  10.9 us (24%)
  waiting for transfers between devices  3.96 us (9%)
  local copies, waits for them, and re-layouts  1.74 us (4%)
    all_to_all x1, blocking collectives, on_device(): sums = lax.all_to_all(sums, 'ch', 0, 0, tiled=True)  14.6 us
    pallas_call x5, Pallas kernels, call(): pl.pallas_call(kernel, out_shape=out_shape, in_specs=[smem] * scalars + [...  9.94 us
    all_to_all x1, starting transfers between devices, on_device(): states = lax.all_to_all(spread, 'ctx', 0, 0, tiled=True)  7.42 us
    ppermute x2, starting transfers between devices, from_behind(): lax.ppermute(block, axis, [(i - 1, i) for i in range(1, lax.axis_size(axi...  6.52 us
    all_to_all x1, waiting for transfers between devices, on_device(): states = lax.all_to_all(spread, 'ctx', 0, 0, tiled=True)  3.96 us
    unnamed x14, local copies, waits for them, and re-layouts  1.73 us
    pallas_call x1, Pallas kernels, on_device(): pl.pallas_call(norm_kernel, out_shape=shape((rows, chans), BF16), compile...  0.91 us
  transfers between devices with their start and end apart: 3, of which 1 were waited for; matrix products, arithmetic and copies ran while one was open for 0% of the time, Pallas kernels for 20%

profile of v4, /device:TPU:1, one launch (start us, length us, event | category | flops | bytes accessed | tf_op | source)
XLA Modules:
  0.0 45.2 jit_solution(10783210741465184325)
XLA Ops:
  0.0 0.0 copy-start
  0.0 1.1 %copy-done = bf16[3,192,512]{2,1,0:T(8,128)(2,1)S(1)} copy-done((bf16[3,192,512]{2,1,0:T(8,128)(2,1)S(1)}, bf16[3,192,512]{2,1,0:T(8,128)(2,1)}, u32[]{:S(2)}) %copy-start) | copy-done | bytes 589848
  1.1 0.0 copy-start.6
  1.1 4.6 %collective-permute-start.1 = (bf16[2,16,512]{2,1,0:T(8,128)(2,1)S(1)}, bf16[2,16,512]{2,1,0:T(8,128)(2,1)S(1)}, u32[]{:S(2)}, u32[]{:S(2)}) collective-permute-start(bf16[2,16,512]{2,1,0:T(8,128)(2,1)S(1)} %get-tuple-element.22), channel_id=1, source_target_pairs={{0,8},{8,16},{16,24},{24,32},{32,40},{40,48},{48,56},{56,64},{64,7... | collective-permute-start | bytes 98312 | tf_op jit(solution)/shard_map/ppermute | solution.py:345
  5.7 0.0 copy-done.6
  5.7 0.0 copy-start.1
  5.8 0.6 %features.1 = (bf16[192,512]{1,0:T(8,128)(2,1)S(1)}, bf16[144,512]{1,0:T(8,128)(2,1)S(1)}, f32[2,8,512]{2,1,0:T(8,128)S(1)}) custom-call(bf16[3,192,512]{2,1,0:T(8,128)(2,1)S(1)} %get-tuple-element.19.raw_ref, f32[3,8,512]{2,1,0:T(8,128)S(1)} %pad.4.short_ref), custom_call_target="tpu_custom_call" | custom-call | flops 2000000000 | tf_op jit(solution)/shard_map/features/pallas_call | solution.py:328
  6.3 1.9 %collective-permute-start = (bf16[144,512]{1,0:T(8,128)(2,1)S(1)}, bf16[144,512]{1,0:T(8,128)(2,1)S(1)}, u32[]{:S(2)}, u32[]{:S(2)}) collective-permute-start(bf16[144,512]{1,0:T(8,128)(2,1)S(1)} %get-tuple-element.20), channel_id=1, source_target_pairs={{0,8},{8,16},{16,24},{24,32},{32,40},{40,48},{48,56},{56,64},{64,7... | collective-permute-start | bytes 442376 | tf_op jit(solution)/shard_map/ppermute | solution.py:345
  8.3 0.0 collective-permute-done.1.halo_ref
  8.3 0.0 copy-done.1
  8.3 1.5 %first.1 = (bf16[32,16,512]{2,1,0:T(8,128)(2,1)}, f32[8,512]{1,0:T(8,128)S(1)}) custom-call(s32[1]{0:T(128)} %bitcast.index_ref, bf16[2,16,512]{2,1,0:T(8,128)(2,1)S(1)} %collective-permute-done.1.halo_ref, f32[2,8,512]{2,1,0:T(8,128)S(1)} %get-tuple-element.23.head_ref, f32[3,8,512]{2,1,0:T(8,128)S(1)} %pad.4.short_ref, f32[16,512]{1,0:T(8,128)S(1)} %copy-done.1, ...), custom_call_target="tpu_custom_call" | custom-call | flops 2000000000 | tf_op jit(solution)/shard_map/first/pallas_call | solution.py:328
  9.8 0.0 copy-start.2
  9.8 0.0 copy-start.3
  9.8 0.0 copy-start.5
  9.8 7.4 %all-to-all-start = ((bf16[32,16,512]{2,1,0:T(8,128)(2,1)}), bf16[32,16,512]{2,1,0:T(8,128)(2,1)S(1)}, u32[]{:S(2)}, u32[]{:S(2)}) async-start(bf16[32,16,512]{2,1,0:T(8,128)(2,1)} %get-tuple-element.26), calls=%async_computation | async-start | bytes 1048576 | tf_op jit(solution)/shard_map/all_to_all | solution.py:375
  17.2 0.0 collective-permute-done.tail_ref
  17.3 0.0 copy-start.4
  17.3 0.0 copy-done.2
  17.3 0.0 copy-done.3
  17.3 0.0 copy-done.5
  17.3 0.6 %copy-done.4 = f32[512]{0:T(512)S(1)} copy-done((f32[512]{0:T(512)S(1)}, f32[512]{0:T(512)}, u32[]{:S(2)}) %copy-start.4) | copy-done | bytes 2072
  17.9 7.0 %direct.1 = (bf16[192,512]{1,0:T(8,128)(2,1)S(1)}, f32[16,512]{1,0:T(8,128)S(1)}, f32[192,512]{1,0:T(8,128)S(1)}, f32[2,16,512]{2,1,0:T(8,128)S(1)}, f32[1,512]{1,0:T(1,128)S(1)}) custom-call(bf16[128,512]{1,0:T(8,128)(2,1)S(1)} %copy-done.2, f32[16,512]{1,0:T(8,128)S(1)} %copy-done.1, f32[16,512]{1,0:T(8,128)S(1)} %copy-done.3, f32[1,512]{1,0:T(1,128)S(1)} %bitcast.4, ...), custom_call_target="tpu_custom_call" | custom-call | flops 8000000000 | tf_op jit(solution)/shard_map/direct/pallas_call | solution.py:328
  24.9 4.0 %all-to-all-done.states_ref = bf16[32,16,512]{2,1,0:T(8,128)(2,1)S(1)} async-done(((bf16[32,16,512]{2,1,0:T(8,128)(2,1)}), bf16[32,16,512]{2,1,0:T(8,128)(2,1)S(1)}, u32[]{:S(2)}, u32[]{:S(2)}) %all-to-all-start) | async-done | bytes 524320 | tf_op jit(solution)/shard_map/all_to_all | solution.py:375
  28.9 0.8 %combine.1 = (f32[192,512]{1,0:T(8,128)S(1)}, f32[8,1,192]{2,1,0:T(1,128)S(1)}) custom-call(s32[1]{0:T(128)} %bitcast.index_ref, f32[16,512]{1,0:T(8,128)S(1)} %get-tuple-element.25.wm_ref, f32[16,512]{1,0:T(8,128)S(1)} %copy-done.1, bf16[32,16,512]{2,1,0:T(8,128)(2,1)S(1)} %all-to-all-done.states_ref, f32[2,16,512]{2,1,0:T(8,128)S(1)} %get-tuple-element.27.lead_ref, ...), custom_call_target="tpu_custom_call" | custom-call | tf_op jit(solution)/shard_map/combine/pallas_call | solution.py:328
  29.7 14.6 %all_to_all.10.sums_ref = f32[8,1,192]{2,1,0:T(1,128)S(1)} all-to-all(f32[8,1,192]{2,1,0:T(1,128)S(1)} %get-tuple-element.32), channel_id=1, replica_groups=mesh['ctx'=32,'ch'=8] {'ch'}, dimensions={0} | all-to-all | bytes 12288 | tf_op jit(solution)/shard_map/all_to_all | solution.py:404
  44.3 0.9 %norm.1 = bf16[192,512]{1,0:T(8,128)(2,1)} custom-call(f32[192,512]{1,0:T(8,128)S(1)} %get-tuple-element.31.gated_ref, f32[8,1,192]{2,1,0:T(1,128)S(1)} %all_to_all.10.sums_ref), custom_call_target="tpu_custom_call" | custom-call | tf_op jit(solution)/shard_map/norm/pallas_call | solution.py:405
  (2 shorter events, 0.0 us)
Async XLA Ops:
  0.0 1.1 %copy-start = (bf16[3,192,512]{2,1,0:T(8,128)(2,1)S(1)}, bf16[3,192,512]{2,1,0:T(8,128)(2,1)}, u32[]{:S(2)}) copy-start(bf16[3,192,512]{2,1,0:T(8,128)(2,1)} %proj_ref.1) | copy-start | bytes 1769476
  1.1 4.7 %copy-start.6 = (f32[7,3,512]{2,0,1:T(8,128)S(1)}, f32[7,3,512]{2,0,1:T(8,128)}, u32[]{:S(2)}) copy-start(f32[7,3,512]{2,0,1:T(8,128)} %param.8) | copy-start | bytes 129028
  1.1 7.2 %collective-permute-start.1 = (bf16[2,16,512]{2,1,0:T(8,128)(2,1)S(1)}, bf16[2,16,512]{2,1,0:T(8,128)(2,1)S(1)}, u32[]{:S(2)}, u32[]{:S(2)}) collective-permute-start(bf16[2,16,512]{2,1,0:T(8,128)(2,1)S(1)} %get-tuple-element.22), channel_id=1, source_target_pairs={{0,8},{8,16},{16,24},{24,32},{32,40},{40,48},{48,56},{56,64},{64,7... | collective-permute-start | bytes 98312 | tf_op jit(solution)/shard_map/ppermute | solution.py:345
  5.7 2.5 %copy-start.1 = (f32[16,512]{1,0:T(8,128)S(1)}, f32[16,512]{1,0:T(8,128)}, u32[]{:S(2)}) copy-start(f32[16,512]{1,0:T(8,128)} %decay_ref.5) | copy-start | bytes 98308
  6.3 10.9 %collective-permute-start = (bf16[144,512]{1,0:T(8,128)(2,1)S(1)}, bf16[144,512]{1,0:T(8,128)(2,1)S(1)}, u32[]{:S(2)}, u32[]{:S(2)}) collective-permute-start(bf16[144,512]{1,0:T(8,128)(2,1)S(1)} %get-tuple-element.20), channel_id=1, source_target_pairs={{0,8},{8,16},{16,24},{24,32},{32,40},{40,48},{48,56},{56,64},{64,7... | collective-permute-start | bytes 442376 | tf_op jit(solution)/shard_map/ppermute | solution.py:345
  9.8 7.5 %copy-start.2 = (bf16[128,512]{1,0:T(8,128)(2,1)S(1)}, bf16[128,512]{1,0:T(8,128)(2,1)}, u32[]{:S(2)}) copy-start(bf16[128,512]{1,0:T(8,128)(2,1)} %med_ref.1) | copy-start | bytes 393220
  9.8 7.5 %copy-start.3 = (f32[16,512]{1,0:T(8,128)S(1)}, f32[16,512]{1,0:T(8,128)}, u32[]{:S(2)}) copy-start(f32[16,512]{1,0:T(8,128)} %res_ref.1) | copy-start | bytes 98308
  9.8 7.5 %copy-start.5 = (f32[512]{0:T(512)S(1)}, f32[512]{0:T(512)}, u32[]{:S(2)}) copy-start(f32[512]{0:T(512)} %param.13) | copy-start | bytes 6148
  9.8 19.0 %all-to-all-start = ((bf16[32,16,512]{2,1,0:T(8,128)(2,1)}), bf16[32,16,512]{2,1,0:T(8,128)(2,1)S(1)}, u32[]{:S(2)}, u32[]{:S(2)}) async-start(bf16[32,16,512]{2,1,0:T(8,128)(2,1)} %get-tuple-element.26), calls=%async_computation | async-start | bytes 1048576 | tf_op jit(solution)/shard_map/all_to_all | solution.py:375
  17.3 0.7 %copy-start.4 = (f32[512]{0:T(512)S(1)}, f32[512]{0:T(512)}, u32[]{:S(2)}) copy-start(f32[512]{0:T(512)} %param.12) | copy-start | bytes 6148

commit v5 on v4

--- a/solution.py
+++ b/solution.py
@@ -89,7 +89,8 @@
         cols = lanes_of(group)
         feats = []
         for j in range(2):
-            ext[group, j, 0:TILE] = halo_ref[j, :, cols].astype(F32)[EDGE - TILE :]
+            before = halo_ref[j, :, cols].astype(F32)[EDGE - TILE :]
+            ext[group, j, 0:TILE] = jnp.where(index_ref[0] > 0, before, 0.0)
             ext[group, j, TILE:] = jnp.zeros((TILE, LANES), F32)
             total = head_ref[j, :, cols] + short_sum(ext.at[group, j], short_ref[1 + j, :, cols], TILE, TILE, 1)
             feats.append(total.astype(BF16).astype(F32))
@@ -159,8 +160,8 @@
             acc[tiles + half * out + i] = acc[tiles + half * out + i] + both * mid[i - j]
 
 
-def direct_kernel(med_ref, decay_ref, res_ref, skip_ref, gain_ref, short_ref, tail_ref, raw_ref, p_ref, first_ref,
-                  q_ref, wm_ref, near_ref, sums_ref, held_ref, med_f32, shifted, signal, pairs, ext):
+def direct_kernel(index_ref, med_ref, decay_ref, res_ref, skip_ref, gain_ref, short_ref, tail_ref, raw_ref, p_ref, first_ref,
+                  q_ref, base_ref, spans_ref, near_ref, sums_ref, held_ref, med_f32, shifted, signal, pairs, ext):
     row_count = p_ref.shape[0]
     out_tiles = row_count // TILE
     block_tiles = BLOCK // TILE
@@ -176,6 +177,9 @@
         decay = decay_ref[:, cols]
         weights = res_ref[:, cols] * jnp.sqrt(one_minus_exp(2.0 * decay))
         eight = jnp.exp(-TILE * decay)
+        spans_ref[0, :, cols] = jnp.exp(-float(row_count) * decay)
+        spans_ref[1, :, cols] = jnp.exp(-float(BLOCK) * decay)
+        spans_ref[2, :, cols] = eight
         med = med_ref[:, cols].astype(F32)
         med_f32[...] = med
         near = [jnp.zeros((TILE, LANES), F32) for _ in range(med_tiles)]
@@ -191,7 +195,7 @@
                 term = term * step
                 state = state * step + med[TILE * i : TILE * (i + 1)]
             reach_weight = jnp.sum(state * jnp.exp(-rate * (TILE - 1 - rows)), axis=0, keepdims=True) * weight
-            wm_ref[n : n + 1, cols] = reach_weight
+            base_ref[TILE * n : TILE * (n + 1), cols] = reach_weight * jnp.exp(-rate * (rows + 2))
             term = reach_weight * jnp.exp(-rate * (rows + 1))
             for i in range(far_tiles):
                 far[i] = far[i] + term
@@ -216,7 +220,7 @@
         for s in range(TILE):
             shifted[s, 0:TILE] = jnp.zeros((TILE, LANES), F32)
             shifted[s, s : s + reach] = taps
-        tail = tail_ref[:, cols].astype(F32)
+        tail = jnp.where(index_ref[0] > 0, tail_ref[:, cols].astype(F32), 0.0)
         lead = tail[0:MED]
         ext[0:TILE] = tail[MED + EDGE - TILE :]
         ext[TILE:] = raw_ref[0, :, cols].astype(F32)
@@ -249,36 +253,32 @@
     lax.fori_loop(0, p_ref.shape[1] // LANES, group_body, 0)
 
 
-def combine_kernel(index_ref, wm_ref, decay_ref, states_ref, lead_ref, near_ref, q_ref, gain_ref,
+def combine_kernel(index_ref, base_ref, spans_ref, states_ref, lead_ref, near_ref, q_ref, gain_ref,
                    gated_ref, sums_ref, entry, squares):
-    row_count = q_ref.shape[0]
     block_tiles = BLOCK // TILE
     own = index_ref[0]
     squares[...] = jnp.zeros(squares.shape, F32)
-    span = jnp.exp(-float(row_count) * decay_ref[...])
-    block_span = jnp.exp(-float(BLOCK) * decay_ref[...])
+    span, block_span = spans_ref[0], spans_ref[1]
 
     def carry_body(j, carried):
         return carried * span + states_ref[j].astype(F32)
 
     carried = lax.fori_loop(0, own - 1, carry_body, jnp.zeros(span.shape, F32))
     part = states_ref[jnp.maximum(own - 1, 0)].astype(F32)
-    state = jnp.where(own > 0, part, 0.0) + jnp.exp(-float(row_count - MED) * decay_ref[...]) * carried
+    state = jnp.where(own > 0, part, 0.0) + block_span * carried
     for b in range(entry.shape[0]):
-        entry[b] = state * wm_ref[...]
+        entry[b] = state
         if b < lead_ref.shape[0]:
             state = state * block_span + lead_ref[b]
 
     def group_body(group, _):
         cols = lanes_of(group)
-        rows = row_iota()
-        decay = decay_ref[:, cols]
-        eight = jnp.exp(-TILE * decay)
+        eight = spans_ref[2, :, cols]
         acc = tiles_of(near_ref[:, cols])
         for n in range(MODES):
             step = jnp.broadcast_to(eight[n : n + 1], (TILE, LANES))
-            powers = jnp.exp(-decay[n : n + 1] * (rows + 2))
-            terms = [entry[b, n : n + 1, cols] * powers for b in range(entry.shape[0])]
+            base = base_ref[TILE * n : TILE * (n + 1), cols]
+            terms = [entry[b, n : n + 1, cols] * base for b in range(entry.shape[0])]
             for i in range(block_tiles):
                 for b in range(entry.shape[0]):
                     acc[b * block_tiles + i] = acc[b * block_tiles + i] + terms[b]
@@ -290,9 +290,11 @@
         return 0
 
     lax.fori_loop(0, q_ref.shape[1] // LANES, group_body, 0)
+    high = squares[...].astype(BF16)
+    low = (squares[...] - high.astype(F32)).astype(BF16)
     sums = lax.dot_general(
-        jnp.ones((TILE, LANES), F32), squares[...], (((1,), (1,)), ((), ())),
-        precision=lax.Precision.HIGHEST, preferred_element_type=F32,
+        jnp.ones((TILE, 2 * LANES), BF16), jnp.concatenate([high, low], 1), (((1,), (1,)), ((), ())),
+        preferred_element_type=F32,
     )
     for i in range(sums_ref.shape[0]):
         sums_ref[i] = sums[0:1]
@@ -305,18 +307,6 @@
     scale = jnp.broadcast_to(lax.rsqrt(total / C + EPS), (TILE, total.shape[1]))
     scale = jnp.transpose(scale)[:, 0:1]
     out_ref[...] = (gated_ref[...] * scale).astype(BF16)
-
-
-def shape(dims, dtype):
-    return jax.ShapeDtypeStruct(dims, dtype)
-
-
-def cost(flops):
-    return pl.CostEstimate(flops=int(flops), bytes_accessed=0, transcendentals=0)
-
-
-def from_behind(block, axis):
-    return lax.ppermute(block, axis, [(i - 1, i) for i in range(1, lax.axis_size(axis))])
 
 
 def shape(dims, dtype=F32):
@@ -342,7 +332,8 @@
 
 
 def from_behind(block, axis):
-    return lax.ppermute(block, axis, [(i - 1, i) for i in range(1, lax.axis_size(axis))])
+    size = lax.axis_size(axis)
+    return lax.ppermute(block, axis, [(i, (i + 1) % size) for i in range(size)])
 
 
 def on_device(projected, short_filter, medium_filter, decay, residues, skip_gain, out_gain):
@@ -373,12 +364,13 @@
         cost=cost(2e9),
     )
     states = lax.all_to_all(spread, "ctx", 0, 0, tiled=True)
-    queries, reach_weights, near, lead, out_gain = call(
+    queries, base, spans, near, lead, out_gain = call(
         direct_kernel,
         "direct",
         (
             shape((rows, chans), BF16),
-            shape((MODES, chans)),
+            shape((MODES * TILE, chans)),
+            shape((3, MODES, chans)),
             shape((rows, chans)),
             shape((MED // BLOCK, MODES, chans)),
             shape((1, chans)),
@@ -390,7 +382,8 @@
             ((MED + rows) // 2, LANES),
             (rows + TILE, LANES),
         ],
-        (medium_filter, decay, residues, skip_gain[None], out_gain[None], short, tail, raw, product, first),
+        (index, medium_filter, decay, residues, skip_gain[None], out_gain[None], short, tail, raw, product, first),
+        scalars=1,
         cost=cost(8e9),
     )
     gated, sums = call(
@@ -398,7 +391,7 @@
         "combine",
         (shape((rows, chans)), shape((ch, 1, rows))),
         [(rows // BLOCK, MODES, chans), (rows, LANES)],
-        (index, reach_weights, decay, states, lead, near, queries, out_gain),
+        (index, base, spans, states, lead, near, queries, out_gain),
         scalars=1,
     )
     sums = lax.all_to_all(sums, "ch", 0, 0, tiled=True)

time: 45.6 us -> 43 us (0.943)
  blocking collectives: 14.6 us -> 13 us
  starting transfers between devices: 13.9 us -> 13 us
    ppermute x2, starting transfers between devices: 6.52 us -> 3.51 us  [from_behind(): return lax.ppermute(block, axis, [(i, (i + 1) % size) for i in range(size)])]
    all_to_all x1, starting transfers between devices: 7.42 us -> 9.54 us  [on_device(): states = lax.all_to_all(spread, 'ctx', 0, 0, tiled=True)]
    all_to_all x1, blocking collectives: 14.6 us -> 13 us  [on_device(): sums = lax.all_to_all(sums, 'ch', 0, 0, tiled=True)]
  transfers between devices with their start and end apart: 3 -> 3, of which waited for: 1 -> 1; matrix products, arithmetic and copies ran while one was open for 0% -> 0% of each run, Pallas kernels for 20% -> 21%
where the time goes in v5:
time: 43 us; the launch traced here: 42.6 us
  starting transfers between devices  13 us (30%)
  blocking collectives  13 us (30%)
  Pallas kernels  10.8 us (25%)
  waiting for transfers between devices  4.01 us (9%)
  local copies, waits for them, and re-layouts  1.74 us (4%)
    all_to_all x1, blocking collectives, on_device(): sums = lax.all_to_all(sums, 'ch', 0, 0, tiled=True)  13 us
    pallas_call x5, Pallas kernels, call(): pl.pallas_call(kernel, out_shape=out_shape, in_specs=[smem] * scalars + [...  9.88 us
    all_to_all x1, starting transfers between devices, on_device(): states = lax.all_to_all(spread, 'ctx', 0, 0, tiled=True)  9.54 us
    all_to_all x1, waiting for transfers between devices, on_device(): states = lax.all_to_all(spread, 'ctx', 0, 0, tiled=True)  4.01 us
    ppermute x2, starting transfers between devices, from_behind(): return lax.ppermute(block, axis, [(i, (i + 1) % size) for i in range(size)])  3.51 us
    unnamed x14, local copies, waits for them, and re-layouts  1.73 us
    pallas_call x1, Pallas kernels, on_device(): pl.pallas_call(norm_kernel, out_shape=shape((rows, chans), BF16), compile...  0.91 us
  transfers between devices with their start and end apart: 3, of which 1 were waited for; matrix products, arithmetic and copies ran while one was open for 0% of the time, Pallas kernels for 21%

profile of v5, /device:TPU:1, one launch (start us, length us, event | category | flops | bytes accessed | tf_op | source)
XLA Modules:
  0.0 42.6 jit_solution(2579705553076665259)
XLA Ops:
  0.0 0.0 copy-start
  0.0 1.1 %copy-done = bf16[3,192,512]{2,1,0:T(8,128)(2,1)S(1)} copy-done((bf16[3,192,512]{2,1,0:T(8,128)(2,1)S(1)}, bf16[3,192,512]{2,1,0:T(8,128)(2,1)}, u32[]{:S(2)}) %copy-start) | copy-done | bytes 589848
  1.1 0.0 copy-start.6
  1.1 2.8 %collective-permute-start.1 = (bf16[2,16,512]{2,1,0:T(8,128)(2,1)S(1)}, bf16[2,16,512]{2,1,0:T(8,128)(2,1)S(1)}, u32[]{:S(2)}, u32[]{:S(2)}) collective-permute-start(bf16[2,16,512]{2,1,0:T(8,128)(2,1)S(1)} %get-tuple-element.23), channel_id=1, source_target_pairs={{0,8},{8,16},{16,24},{24,32},{32,40},{40,48},{48,56},{56,64},{64,7... | collective-permute-start | bytes 98312 | tf_op jit(solution)/shard_map/ppermute | solution.py:336
  3.9 0.0 copy-done.6
  3.9 0.0 copy-start.2
  3.9 0.6 %features.1 = (bf16[192,512]{1,0:T(8,128)(2,1)S(1)}, bf16[144,512]{1,0:T(8,128)(2,1)S(1)}, f32[2,8,512]{2,1,0:T(8,128)S(1)}) custom-call(bf16[3,192,512]{2,1,0:T(8,128)(2,1)S(1)} %get-tuple-element.20.raw_ref, f32[3,8,512]{2,1,0:T(8,128)S(1)} %pad.4.short_ref), custom_call_target="tpu_custom_call" | custom-call | flops 2000000000 | tf_op jit(solution)/shard_map/features/pallas_call | solution.py:318
  4.5 0.7 %collective-permute-start = (bf16[144,512]{1,0:T(8,128)(2,1)S(1)}, bf16[144,512]{1,0:T(8,128)(2,1)S(1)}, u32[]{:S(2)}, u32[]{:S(2)}) collective-permute-start(bf16[144,512]{1,0:T(8,128)(2,1)S(1)} %get-tuple-element.21), channel_id=1, source_target_pairs={{0,8},{8,16},{16,24},{24,32},{32,40},{40,48},{48,56},{56,64},{64,7... | collective-permute-start | bytes 442376 | tf_op jit(solution)/shard_map/ppermute | solution.py:336
  5.2 0.0 collective-permute-done.1.halo_ref
  5.2 0.0 copy-done.2
  5.2 1.5 %first.1 = (bf16[32,16,512]{2,1,0:T(8,128)(2,1)}, f32[8,512]{1,0:T(8,128)S(1)}) custom-call(s32[1]{0:T(128)} %bitcast.index_ref, bf16[2,16,512]{2,1,0:T(8,128)(2,1)S(1)} %collective-permute-done.1.halo_ref, f32[2,8,512]{2,1,0:T(8,128)S(1)} %get-tuple-element.24.head_ref, f32[3,8,512]{2,1,0:T(8,128)S(1)} %pad.4.short_ref, f32[16,512]{1,0:T(8,128)S(1)} %copy-done.2, ...), custom_call_target="tpu_custom_call" | custom-call | flops 2000000000 | tf_op jit(solution)/shard_map/first/pallas_call | solution.py:318
  6.7 0.0 copy-start.1
  6.8 0.0 copy-start.3
  6.8 0.0 copy-start.5
  6.8 9.5 %all-to-all-start = ((bf16[32,16,512]{2,1,0:T(8,128)(2,1)}), bf16[32,16,512]{2,1,0:T(8,128)(2,1)S(1)}, u32[]{:S(2)}, u32[]{:S(2)}) async-start(bf16[32,16,512]{2,1,0:T(8,128)(2,1)} %get-tuple-element.28), calls=%async_computation | async-start | bytes 1048576 | tf_op jit(solution)/shard_map/all_to_all | solution.py:366
  16.3 0.0 collective-permute-done.tail_ref
  16.3 0.0 copy-start.4
  16.3 0.0 copy-done.1
  16.3 0.0 copy-done.3
  16.3 0.0 copy-done.5
  16.4 0.6 %copy-done.4 = f32[512]{0:T(512)S(1)} copy-done((f32[512]{0:T(512)S(1)}, f32[512]{0:T(512)}, u32[]{:S(2)}) %copy-start.4) | copy-done | bytes 2072
  17.0 7.0 %direct.1 = (bf16[192,512]{1,0:T(8,128)(2,1)S(1)}, f32[128,512]{1,0:T(8,128)S(1)}, f32[3,16,512]{2,1,0:T(8,128)S(1)}, f32[192,512]{1,0:T(8,128)S(1)}, f32[2,16,512]{2,1,0:T(8,128)S(1)}, /*index=5*/f32[1,512]{1,0:T(1,128)S(1)}) custom-call(s32[1]{0:T(128)} %bitcast.index_ref, bf16[128,512]{1,0:T(8,128)(2,1)S(1)} %copy-done.1, f32[16,512]{1,0:T(8,128)S(1)} %copy-done.2, ...), custom_call_target="tpu_custom_call" | custom-call | flops 8000000000 | tf_op jit(solution)/shard_map/direct/pallas_call | solution.py:318
  24.0 4.0 %all-to-all-done.states_ref = bf16[32,16,512]{2,1,0:T(8,128)(2,1)S(1)} async-done(((bf16[32,16,512]{2,1,0:T(8,128)(2,1)}), bf16[32,16,512]{2,1,0:T(8,128)(2,1)S(1)}, u32[]{:S(2)}, u32[]{:S(2)}) %all-to-all-start) | async-done | bytes 524320 | tf_op jit(solution)/shard_map/all_to_all | solution.py:366
  28.0 0.7 %combine.1 = (f32[192,512]{1,0:T(8,128)S(1)}, f32[8,1,192]{2,1,0:T(1,128)S(1)}) custom-call(s32[1]{0:T(128)} %bitcast.index_ref, f32[128,512]{1,0:T(8,128)S(1)} %get-tuple-element.26.base_ref, f32[3,16,512]{2,1,0:T(8,128)S(1)} %get-tuple-element.27.spans_ref, bf16[32,16,512]{2,1,0:T(8,128)(2,1)S(1)} %all-to-all-done.states_ref, ...), custom_call_target="tpu_custom_call" | custom-call | tf_op jit(solution)/shard_map/combine/pallas_call | solution.py:318
  28.8 13.0 %all_to_all.10.sums_ref = f32[8,1,192]{2,1,0:T(1,128)S(1)} all-to-all(f32[8,1,192]{2,1,0:T(1,128)S(1)} %get-tuple-element.34), channel_id=1, replica_groups=mesh['ctx'=32,'ch'=8] {'ch'}, dimensions={0} | all-to-all | bytes 12288 | tf_op jit(solution)/shard_map/all_to_all | solution.py:397
  41.7 0.9 %norm.1 = bf16[192,512]{1,0:T(8,128)(2,1)} custom-call(f32[192,512]{1,0:T(8,128)S(1)} %get-tuple-element.33.gated_ref, f32[8,1,192]{2,1,0:T(1,128)S(1)} %all_to_all.10.sums_ref), custom_call_target="tpu_custom_call" | custom-call | tf_op jit(solution)/shard_map/norm/pallas_call | solution.py:398
  (2 shorter events, 0.0 us)
Async XLA Ops:
  0.0 1.1 %copy-start = (bf16[3,192,512]{2,1,0:T(8,128)(2,1)S(1)}, bf16[3,192,512]{2,1,0:T(8,128)(2,1)}, u32[]{:S(2)}) copy-start(bf16[3,192,512]{2,1,0:T(8,128)(2,1)} %proj_ref.1) | copy-start | bytes 1769476
  1.1 2.8 %copy-start.6 = (f32[7,3,512]{2,0,1:T(8,128)S(1)}, f32[7,3,512]{2,0,1:T(8,128)}, u32[]{:S(2)}) copy-start(f32[7,3,512]{2,0,1:T(8,128)} %param.8) | copy-start | bytes 129028
  1.1 4.1 %collective-permute-start.1 = (bf16[2,16,512]{2,1,0:T(8,128)(2,1)S(1)}, bf16[2,16,512]{2,1,0:T(8,128)(2,1)S(1)}, u32[]{:S(2)}, u32[]{:S(2)}) collective-permute-start(bf16[2,16,512]{2,1,0:T(8,128)(2,1)S(1)} %get-tuple-element.23), channel_id=1, source_target_pairs={{0,8},{8,16},{16,24},{24,32},{32,40},{40,48},{48,56},{56,64},{64,7... | collective-permute-start | bytes 98312 | tf_op jit(solution)/shard_map/ppermute | solution.py:336
  3.9 1.3 %copy-start.2 = (f32[16,512]{1,0:T(8,128)S(1)}, f32[16,512]{1,0:T(8,128)}, u32[]{:S(2)}) copy-start(f32[16,512]{1,0:T(8,128)} %decay_ref.3) | copy-start | bytes 98308
  4.5 11.8 %collective-permute-start = (bf16[144,512]{1,0:T(8,128)(2,1)S(1)}, bf16[144,512]{1,0:T(8,128)(2,1)S(1)}, u32[]{:S(2)}, u32[]{:S(2)}) collective-permute-start(bf16[144,512]{1,0:T(8,128)(2,1)S(1)} %get-tuple-element.21), channel_id=1, source_target_pairs={{0,8},{8,16},{16,24},{24,32},{32,40},{40,48},{48,56},{56,64},{64,7... | collective-permute-start | bytes 442376 | tf_op jit(solution)/shard_map/ppermute | solution.py:336
  6.7 9.6 %copy-start.1 = (bf16[128,512]{1,0:T(8,128)(2,1)S(1)}, bf16[128,512]{1,0:T(8,128)(2,1)}, u32[]{:S(2)}) copy-start(bf16[128,512]{1,0:T(8,128)(2,1)} %med_ref.1) | copy-start | bytes 393220
  6.8 9.6 %copy-start.3 = (f32[16,512]{1,0:T(8,128)S(1)}, f32[16,512]{1,0:T(8,128)}, u32[]{:S(2)}) copy-start(f32[16,512]{1,0:T(8,128)} %res_ref.1) | copy-start | bytes 98308
  6.8 9.6 %copy-start.5 = (f32[512]{0:T(512)S(1)}, f32[512]{0:T(512)}, u32[]{:S(2)}) copy-start(f32[512]{0:T(512)} %param.13) | copy-start | bytes 6148
  6.8 21.3 %all-to-all-start = ((bf16[32,16,512]{2,1,0:T(8,128)(2,1)}), bf16[32,16,512]{2,1,0:T(8,128)(2,1)S(1)}, u32[]{:S(2)}, u32[]{:S(2)}) async-start(bf16[32,16,512]{2,1,0:T(8,128)(2,1)} %get-tuple-element.28), calls=%async_computation | async-start | bytes 1048576 | tf_op jit(solution)/shard_map/all_to_all | solution.py:366
  16.3 0.7 %copy-start.4 = (f32[512]{0:T(512)S(1)}, f32[512]{0:T(512)}, u32[]{:S(2)}) copy-start(f32[512]{0:T(512)} %param.12) | copy-start | bytes 6148

commit v6 on v5

--- a/solution.py
+++ b/solution.py
@@ -1,3 +1,4 @@
+import functools
 import jax
 import jax.numpy as jnp
 from jax import lax
@@ -81,9 +82,31 @@
     lax.fori_loop(0, p_ref.shape[1] // LANES, group_body, 0)
 
 
-def first_kernel(index_ref, halo_ref, head_ref, short_ref, decay_ref, p_ref, spread_ref, first_ref, ext):
+def state_kernel(p_ref, decay_ref, sums_ref):
+    part_tiles = (p_ref.shape[0] - MED) // TILE
+
+    def group_body(group, _):
+        cols = lanes_of(group)
+        rows = row_iota()
+        tiles = tiles_of(p_ref[:, cols].astype(F32))
+        decay = decay_ref[:, cols]
+        eight = jnp.exp(-TILE * decay)
+        for n in range(MODES):
+            step = jnp.broadcast_to(eight[n : n + 1], (TILE, LANES))
+            close = jnp.exp(-decay[n : n + 1] * (TILE - 1 - rows))
+            state = tiles[1]
+            for i in range(2, len(tiles)):
+                if i == part_tiles:
+                    sums_ref[1, n : n + 1, cols] = jnp.sum(state * close, axis=0, keepdims=True)
+                state = state * step + tiles[i]
+            sums_ref[0, n : n + 1, cols] = jnp.sum(state * close, axis=0, keepdims=True)
+        return 0
+
+    lax.fori_loop(0, p_ref.shape[1] // LANES, group_body, 0)
+
+
+def first_kernel(index_ref, halo_ref, head_ref, short_ref, decay_ref, sums_ref, spread_ref, first_ref, ext, *, row_count):
     following = jnp.minimum(index_ref[0] + 1, spread_ref.shape[0] - 1)
-    part_tiles = (p_ref.shape[0] - MED) // TILE
 
     def group_body(group, _):
         cols = lanes_of(group)
@@ -96,23 +119,14 @@
             feats.append(total.astype(BF16).astype(F32))
         product = (feats[0] * feats[1]).astype(BF16).astype(F32)
         first_ref[:, cols] = product
-        tiles = tiles_of(p_ref[:, cols].astype(F32))
         decay = decay_ref[:, cols]
-        eight = jnp.exp(-TILE * decay)
-        wholes, parts = [], []
-        for n in range(MODES):
-            step = jnp.broadcast_to(eight[n : n + 1], (TILE, LANES))
-            close = jnp.exp(-decay[n : n + 1] * (TILE - 1 - row_iota()))
-            state = product
-            for i in range(1, len(tiles)):
-                if i == part_tiles:
-                    parts.append(jnp.sum(state * close, axis=0, keepdims=True))
-                state = state * step + tiles[i]
-            wholes.append(jnp.sum(state * close, axis=0, keepdims=True))
-        whole = jnp.concatenate(wholes, 0).astype(BF16)
+        own = modal_sums([product], decay, row_iota())
+        whole = sums_ref[0, :, cols] + own * jnp.exp(-float(row_count - TILE) * decay)
+        part = sums_ref[1, :, cols] + own * jnp.exp(-float(row_count - MED - TILE) * decay)
+        whole = whole.astype(BF16)
         for i in range(spread_ref.shape[0]):
             spread_ref[i, :, cols] = whole
-        spread_ref[following, :, cols] = jnp.concatenate(parts, 0).astype(BF16)
+        spread_ref[following, :, cols] = part.astype(BF16)
         return 0
 
     lax.fori_loop(0, spread_ref.shape[2] // LANES, group_body, 0, unroll=True)
@@ -354,12 +368,13 @@
         cost=cost(2e9),
     )
     tail = from_behind(tail, "ctx")
+    partial = call(state_kernel, "states", shape((2, MODES, chans)), [], (product, decay), cost=cost(1e9))
     spread, first = call(
-        first_kernel,
+        functools.partial(first_kernel, row_count=rows),
         "first",
         (shape((ctx, MODES, chans), BF16), shape((TILE, chans))),
         [(chans // LANES, 2, 2 * TILE, LANES)],
-        (index, halo, head, short, decay, product),
+        (index, halo, head, short, decay, partial),
         scalars=1,
         cost=cost(2e9),
     )

time: 43 us -> 42.5 us (0.988)
  starting transfers between devices: 13 us -> 12.3 us
    all_to_all x1, starting transfers between devices: 9.54 us -> 8.83 us  [on_device(): states = lax.all_to_all(spread, 'ctx', 0, 0, tiled=True)]
    pallas_call x5 -> x6, Pallas kernels: 9.88 us -> 10.1 us  [call(): pl.pallas_call(kernel, out_shape=out_shape, in_specs=[smem] * scalars + [...]
  transfers between devices with their start and end apart: 3 -> 3, of which waited for: 1 -> 1; matrix products, arithmetic and copies ran while one was open for 0% -> 0% of each run, Pallas kernels for 21% -> 22%
where the time goes in v6:
time: 42.5 us; the launch traced here: 42.1 us
  blocking collectives  13 us (31%)
  starting transfers between devices  12.3 us (29%)
  Pallas kernels  11 us (26%)
  waiting for transfers between devices  4.01 us (9%)
  local copies, waits for them, and re-layouts  1.74 us (4%)
    all_to_all x1, blocking collectives, on_device(): sums = lax.all_to_all(sums, 'ch', 0, 0, tiled=True)  13 us
    pallas_call x6, Pallas kernels, call(): pl.pallas_call(kernel, out_shape=out_shape, in_specs=[smem] * scalars + [...  10.1 us
    all_to_all x1, starting transfers between devices, on_device(): states = lax.all_to_all(spread, 'ctx', 0, 0, tiled=True)  8.83 us
    all_to_all x1, waiting for transfers between devices, on_device(): states = lax.all_to_all(spread, 'ctx', 0, 0, tiled=True)  4.01 us
    ppermute x2, starting transfers between devices, from_behind(): return lax.ppermute(block, axis, [(i, (i + 1) % size) for i in range(size)])  3.51 us
    unnamed x14, local copies, waits for them, and re-layouts  1.73 us
    pallas_call x1, Pallas kernels, on_device(): pl.pallas_call(norm_kernel, out_shape=shape((rows, chans), BF16), compile...  0.91 us
  transfers between devices with their start and end apart: 3, of which 1 were waited for; matrix products, arithmetic and copies ran while one was open for 0% of the time, Pallas kernels for 22%

profile of v6, /device:TPU:1, one launch (start us, length us, event | category | flops | bytes accessed | tf_op | source)
XLA Modules:
  0.0 42.1 jit_solution(1482600282739597236)
XLA Ops:
  0.0 0.0 copy-start
  0.0 1.1 %copy-done = bf16[3,192,512]{2,1,0:T(8,128)(2,1)S(1)} copy-done((bf16[3,192,512]{2,1,0:T(8,128)(2,1)S(1)}, bf16[3,192,512]{2,1,0:T(8,128)(2,1)}, u32[]{:S(2)}) %copy-start) | copy-done | bytes 589848
  1.1 0.0 copy-start.6
  1.1 2.8 %collective-permute-start.1 = (bf16[2,16,512]{2,1,0:T(8,128)(2,1)S(1)}, bf16[2,16,512]{2,1,0:T(8,128)(2,1)S(1)}, u32[]{:S(2)}, u32[]{:S(2)}) collective-permute-start(bf16[2,16,512]{2,1,0:T(8,128)(2,1)S(1)} %get-tuple-element.23), channel_id=1, source_target_pairs={{0,8},{8,16},{16,24},{24,32},{32,40},{40,48},{48,56},{56,64},{64,7... | collective-permute-start | bytes 98312 | tf_op jit(solution)/shard_map/ppermute | solution.py:350
  3.9 0.0 copy-done.6
  3.9 0.0 copy-start.2
  3.9 0.6 %features.1 = (bf16[192,512]{1,0:T(8,128)(2,1)S(1)}, bf16[144,512]{1,0:T(8,128)(2,1)S(1)}, f32[2,8,512]{2,1,0:T(8,128)S(1)}) custom-call(bf16[3,192,512]{2,1,0:T(8,128)(2,1)S(1)} %get-tuple-element.20.raw_ref, f32[3,8,512]{2,1,0:T(8,128)S(1)} %pad.4.short_ref), custom_call_target="tpu_custom_call" | custom-call | flops 2000000000 | tf_op jit(solution)/shard_map/features/pallas_call | solution.py:332
  4.5 0.7 %collective-permute-start = (bf16[144,512]{1,0:T(8,128)(2,1)S(1)}, bf16[144,512]{1,0:T(8,128)(2,1)S(1)}, u32[]{:S(2)}, u32[]{:S(2)}) collective-permute-start(bf16[144,512]{1,0:T(8,128)(2,1)S(1)} %get-tuple-element.21), channel_id=1, source_target_pairs={{0,8},{8,16},{16,24},{24,32},{32,40},{40,48},{48,56},{56,64},{64,7... | collective-permute-start | bytes 442376 | tf_op jit(solution)/shard_map/ppermute | solution.py:350
  5.2 0.0 copy-done.2
  5.2 0.7 %states.1.sums_ref = f32[2,16,512]{2,1,0:T(8,128)S(1)} custom-call(bf16[192,512]{1,0:T(8,128)(2,1)S(1)} %get-tuple-element.22.p_ref, f32[16,512]{1,0:T(8,128)S(1)} %copy-done.2), custom_call_target="tpu_custom_call" | custom-call | flops 1000000000 | tf_op jit(solution)/shard_map/states/pallas_call | solution.py:332
  5.9 0.0 collective-permute-done.1.halo_ref
  5.9 1.0 %first.1 = (bf16[32,16,512]{2,1,0:T(8,128)(2,1)}, f32[8,512]{1,0:T(8,128)S(1)}) custom-call(s32[1]{0:T(128)} %bitcast.index_ref, bf16[2,16,512]{2,1,0:T(8,128)(2,1)S(1)} %collective-permute-done.1.halo_ref, f32[2,8,512]{2,1,0:T(8,128)S(1)} %get-tuple-element.24.head_ref, f32[3,8,512]{2,1,0:T(8,128)S(1)} %pad.4.short_ref, f32[16,512]{1,0:T(8,128)S(1)} %copy-done.2, ...), custom_call_target="tpu_custom_call" | custom-call | flops 2000000000 | tf_op jit(solution)/shard_map/first/pallas_call | solution.py:332
  6.9 0.0 copy-start.1
  6.9 0.0 copy-start.3
  6.9 0.0 copy-start.5
  6.9 8.8 %all-to-all-start = ((bf16[32,16,512]{2,1,0:T(8,128)(2,1)}), bf16[32,16,512]{2,1,0:T(8,128)(2,1)S(1)}, u32[]{:S(2)}, u32[]{:S(2)}) async-start(bf16[32,16,512]{2,1,0:T(8,128)(2,1)} %get-tuple-element.28), calls=%async_computation | async-start | bytes 1048576 | tf_op jit(solution)/shard_map/all_to_all | solution.py:381
  15.8 0.0 collective-permute-done.tail_ref
  15.8 0.0 copy-start.4
  15.8 0.0 copy-done.1
  15.8 0.0 copy-done.3
  15.8 0.0 copy-done.5
  15.8 0.6 %copy-done.4 = f32[512]{0:T(512)S(1)} copy-done((f32[512]{0:T(512)S(1)}, f32[512]{0:T(512)}, u32[]{:S(2)}) %copy-start.4) | copy-done | bytes 2072
  16.5 7.0 %direct.1 = (bf16[192,512]{1,0:T(8,128)(2,1)S(1)}, f32[128,512]{1,0:T(8,128)S(1)}, f32[3,16,512]{2,1,0:T(8,128)S(1)}, f32[192,512]{1,0:T(8,128)S(1)}, f32[2,16,512]{2,1,0:T(8,128)S(1)}, /*index=5*/f32[1,512]{1,0:T(1,128)S(1)}) custom-call(s32[1]{0:T(128)} %bitcast.index_ref, bf16[128,512]{1,0:T(8,128)(2,1)S(1)} %copy-done.1, f32[16,512]{1,0:T(8,128)S(1)} %copy-done.2, ...), custom_call_target="tpu_custom_call" | custom-call | flops 8000000000 | tf_op jit(solution)/shard_map/direct/pallas_call | solution.py:332
  23.5 4.0 %all-to-all-done.states_ref = bf16[32,16,512]{2,1,0:T(8,128)(2,1)S(1)} async-done(((bf16[32,16,512]{2,1,0:T(8,128)(2,1)}), bf16[32,16,512]{2,1,0:T(8,128)(2,1)S(1)}, u32[]{:S(2)}, u32[]{:S(2)}) %all-to-all-start) | async-done | bytes 524320 | tf_op jit(solution)/shard_map/all_to_all | solution.py:381
  27.5 0.7 %combine.1 = (f32[192,512]{1,0:T(8,128)S(1)}, f32[8,1,192]{2,1,0:T(1,128)S(1)}) custom-call(s32[1]{0:T(128)} %bitcast.index_ref, f32[128,512]{1,0:T(8,128)S(1)} %get-tuple-element.26.base_ref, f32[3,16,512]{2,1,0:T(8,128)S(1)} %get-tuple-element.27.spans_ref, bf16[32,16,512]{2,1,0:T(8,128)(2,1)S(1)} %all-to-all-done.states_ref, ...), custom_call_target="tpu_custom_call" | custom-call | tf_op jit(solution)/shard_map/combine/pallas_call | solution.py:332
  28.2 13.0 %all_to_all.10.sums_ref = f32[8,1,192]{2,1,0:T(1,128)S(1)} all-to-all(f32[8,1,192]{2,1,0:T(1,128)S(1)} %get-tuple-element.34), channel_id=1, replica_groups=mesh['ctx'=32,'ch'=8] {'ch'}, dimensions={0} | all-to-all | bytes 12288 | tf_op jit(solution)/shard_map/all_to_all | solution.py:412
  41.2 0.9 %norm.1 = bf16[192,512]{1,0:T(8,128)(2,1)} custom-call(f32[192,512]{1,0:T(8,128)S(1)} %get-tuple-element.33.gated_ref, f32[8,1,192]{2,1,0:T(1,128)S(1)} %all_to_all.10.sums_ref), custom_call_target="tpu_custom_call" | custom-call | tf_op jit(solution)/shard_map/norm/pallas_call | solution.py:413
  (2 shorter events, 0.0 us)
Async XLA Ops:
  0.0 1.1 %copy-start = (bf16[3,192,512]{2,1,0:T(8,128)(2,1)S(1)}, bf16[3,192,512]{2,1,0:T(8,128)(2,1)}, u32[]{:S(2)}) copy-start(bf16[3,192,512]{2,1,0:T(8,128)(2,1)} %proj_ref.1) | copy-start | bytes 1769476
  1.1 2.8 %copy-start.6 = (f32[7,3,512]{2,0,1:T(8,128)S(1)}, f32[7,3,512]{2,0,1:T(8,128)}, u32[]{:S(2)}) copy-start(f32[7,3,512]{2,0,1:T(8,128)} %param.8) | copy-start | bytes 129028
  1.1 4.8 %collective-permute-start.1 = (bf16[2,16,512]{2,1,0:T(8,128)(2,1)S(1)}, bf16[2,16,512]{2,1,0:T(8,128)(2,1)S(1)}, u32[]{:S(2)}, u32[]{:S(2)}) collective-permute-start(bf16[2,16,512]{2,1,0:T(8,128)(2,1)S(1)} %get-tuple-element.23), channel_id=1, source_target_pairs={{0,8},{8,16},{16,24},{24,32},{32,40},{40,48},{48,56},{56,64},{64,7... | collective-permute-start | bytes 98312 | tf_op jit(solution)/shard_map/ppermute | solution.py:350
  3.9 1.3 %copy-start.2 = (f32[16,512]{1,0:T(8,128)S(1)}, f32[16,512]{1,0:T(8,128)}, u32[]{:S(2)}) copy-start(f32[16,512]{1,0:T(8,128)} %decay_ref.5) | copy-start | bytes 98308
  4.5 11.3 %collective-permute-start = (bf16[144,512]{1,0:T(8,128)(2,1)S(1)}, bf16[144,512]{1,0:T(8,128)(2,1)S(1)}, u32[]{:S(2)}, u32[]{:S(2)}) collective-permute-start(bf16[144,512]{1,0:T(8,128)(2,1)S(1)} %get-tuple-element.21), channel_id=1, source_target_pairs={{0,8},{8,16},{16,24},{24,32},{32,40},{40,48},{48,56},{56,64},{64,7... | collective-permute-start | bytes 442376 | tf_op jit(solution)/shard_map/ppermute | solution.py:350
  6.9 8.9 %copy-start.1 = (bf16[128,512]{1,0:T(8,128)(2,1)S(1)}, bf16[128,512]{1,0:T(8,128)(2,1)}, u32[]{:S(2)}) copy-start(bf16[128,512]{1,0:T(8,128)(2,1)} %med_ref.1) | copy-start | bytes 393220
  6.9 8.9 %copy-start.3 = (f32[16,512]{1,0:T(8,128)S(1)}, f32[16,512]{1,0:T(8,128)}, u32[]{:S(2)}) copy-start(f32[16,512]{1,0:T(8,128)} %res_ref.1) | copy-start | bytes 98308
  6.9 8.9 %copy-start.5 = (f32[512]{0:T(512)S(1)}, f32[512]{0:T(512)}, u32[]{:S(2)}) copy-start(f32[512]{0:T(512)} %param.13) | copy-start | bytes 6148
  6.9 20.6 %all-to-all-start = ((bf16[32,16,512]{2,1,0:T(8,128)(2,1)}), bf16[32,16,512]{2,1,0:T(8,128)(2,1)S(1)}, u32[]{:S(2)}, u32[]{:S(2)}) async-start(bf16[32,16,512]{2,1,0:T(8,128)(2,1)} %get-tuple-element.28), calls=%async_computation | async-start | bytes 1048576 | tf_op jit(solution)/shard_map/all_to_all | solution.py:381
  15.8 0.7 %copy-start.4 = (f32[512]{0:T(512)S(1)}, f32[512]{0:T(512)}, u32[]{:S(2)}) copy-start(f32[512]{0:T(512)} %param.12) | copy-start | bytes 6148

commit v7 on v6

--- a/solution.py
+++ b/solution.py
@@ -314,15 +314,6 @@
         sums_ref[i] = sums[0:1]
 
 
-def norm_kernel(gated_ref, sums_ref, out_ref):
-    total = sums_ref[0]
-    for i in range(1, sums_ref.shape[0]):
-        total = total + sums_ref[i]
-    scale = jnp.broadcast_to(lax.rsqrt(total / C + EPS), (TILE, total.shape[1]))
-    scale = jnp.transpose(scale)[:, 0:1]
-    out_ref[...] = (gated_ref[...] * scale).astype(BF16)
-
-
 def shape(dims, dtype=F32):
     return jax.ShapeDtypeStruct(dims, dtype)
 
@@ -410,9 +401,8 @@
         scalars=1,
     )
     sums = lax.all_to_all(sums, "ch", 0, 0, tiled=True)
-    return pl.pallas_call(
-        norm_kernel, out_shape=shape((rows, chans), BF16), compiler_params=PARAMS, name="norm"
-    )(gated, sums)
+    scale = lax.rsqrt(jnp.sum(sums, (0, 1)) / C + EPS)
+    return (gated * scale[:, None]).astype(BF16)
 
 
 def solution(mesh):

time: 42.5 us -> 42.4 us (level)
  Pallas kernels: 11 us -> 10.1 us
  other arithmetic: 0 us -> 0.81 us
    pallas_call x1 -> x0, Pallas kernels: 0.91 us -> none  [on_device(): pl.pallas_call(norm_kernel, out_shape=shape((rows, chans), BF16), compile...]
    convert_element_type x0 -> x1, other arithmetic: none -> 0.78 us  [on_device(): return (gated * scale[:, None]).astype(BF16)]
where the time goes in v7:
time: 42.4 us; the launch traced here: 42 us
  blocking collectives  13 us (31%)
  starting transfers between devices  12.3 us (29%)
  Pallas kernels  10.1 us (24%)
  waiting for transfers between devices  4.01 us (9%)
  local copies, waits for them, and re-layouts  1.74 us (4%)
  other arithmetic  0.81 us (2%)
    all_to_all x1, blocking collectives, on_device(): sums = lax.all_to_all(sums, 'ch', 0, 0, tiled=True)  13 us
    pallas_call x6, Pallas kernels, call(): pl.pallas_call(kernel, out_shape=out_shape, in_specs=[smem] * scalars + [...  10.1 us
    all_to_all x1, starting transfers between devices, on_device(): states = lax.all_to_all(spread, 'ctx', 0, 0, tiled=True)  8.84 us
    all_to_all x1, waiting for transfers between devices, on_device(): states = lax.all_to_all(spread, 'ctx', 0, 0, tiled=True)  4.01 us
    ppermute x2, starting transfers between devices, from_behind(): return lax.ppermute(block, axis, [(i, (i + 1) % size) for i in range(size)])  3.51 us
    unnamed x14, local copies, waits for them, and re-layouts  1.73 us
  transfers between devices with their start and end apart: 3, of which 1 were waited for; matrix products, arithmetic and copies ran while one was open for 0% of the time, Pallas kernels for 22%

profile of v7, /device:TPU:1, one launch (start us, length us, event | category | flops | bytes accessed | tf_op | source)
XLA Modules:
  0.0 42.0 jit_solution(2913839731953511490)
XLA Ops:
  0.0 0.0 copy-start
  0.0 1.1 %copy-done = bf16[3,192,512]{2,1,0:T(8,128)(2,1)S(1)} copy-done((bf16[3,192,512]{2,1,0:T(8,128)(2,1)S(1)}, bf16[3,192,512]{2,1,0:T(8,128)(2,1)}, u32[]{:S(2)}) %copy-start) | copy-done | bytes 589848
  1.1 0.0 copy-start.6
  1.1 2.8 %collective-permute-start.1 = (bf16[2,16,512]{2,1,0:T(8,128)(2,1)S(1)}, bf16[2,16,512]{2,1,0:T(8,128)(2,1)S(1)}, u32[]{:S(2)}, u32[]{:S(2)}) collective-permute-start(bf16[2,16,512]{2,1,0:T(8,128)(2,1)S(1)} %get-tuple-element.23), channel_id=1, source_target_pairs={{0,8},{8,16},{16,24},{24,32},{32,40},{40,48},{48,56},{56,64},{64,7... | collective-permute-start | bytes 98312 | tf_op jit(solution)/shard_map/ppermute | solution.py:341
  3.9 0.0 copy-done.6
  3.9 0.0 copy-start.2
  3.9 0.6 %features.1 = (bf16[192,512]{1,0:T(8,128)(2,1)S(1)}, bf16[144,512]{1,0:T(8,128)(2,1)S(1)}, f32[2,8,512]{2,1,0:T(8,128)S(1)}) custom-call(bf16[3,192,512]{2,1,0:T(8,128)(2,1)S(1)} %get-tuple-element.20.raw_ref, f32[3,8,512]{2,1,0:T(8,128)S(1)} %pad.4.short_ref), custom_call_target="tpu_custom_call" | custom-call | flops 2000000000 | tf_op jit(solution)/shard_map/features/pallas_call | solution.py:323
  4.5 0.7 %collective-permute-start = (bf16[144,512]{1,0:T(8,128)(2,1)S(1)}, bf16[144,512]{1,0:T(8,128)(2,1)S(1)}, u32[]{:S(2)}, u32[]{:S(2)}) collective-permute-start(bf16[144,512]{1,0:T(8,128)(2,1)S(1)} %get-tuple-element.21), channel_id=1, source_target_pairs={{0,8},{8,16},{16,24},{24,32},{32,40},{40,48},{48,56},{56,64},{64,7... | collective-permute-start | bytes 442376 | tf_op jit(solution)/shard_map/ppermute | solution.py:341
  5.2 0.0 copy-done.2
  5.2 0.7 %states.1.sums_ref = f32[2,16,512]{2,1,0:T(8,128)S(1)} custom-call(bf16[192,512]{1,0:T(8,128)(2,1)S(1)} %get-tuple-element.22.p_ref, f32[16,512]{1,0:T(8,128)S(1)} %copy-done.2), custom_call_target="tpu_custom_call" | custom-call | flops 1000000000 | tf_op jit(solution)/shard_map/states/pallas_call | solution.py:323
  5.9 0.0 collective-permute-done.1.halo_ref
  5.9 1.0 %first.1 = (bf16[32,16,512]{2,1,0:T(8,128)(2,1)}, f32[8,512]{1,0:T(8,128)S(1)}) custom-call(s32[1]{0:T(128)} %bitcast.index_ref, bf16[2,16,512]{2,1,0:T(8,128)(2,1)S(1)} %collective-permute-done.1.halo_ref, f32[2,8,512]{2,1,0:T(8,128)S(1)} %get-tuple-element.24.head_ref, f32[3,8,512]{2,1,0:T(8,128)S(1)} %pad.4.short_ref, f32[16,512]{1,0:T(8,128)S(1)} %copy-done.2, ...), custom_call_target="tpu_custom_call" | custom-call | flops 2000000000 | tf_op jit(solution)/shard_map/first/pallas_call | solution.py:323
  6.9 0.0 copy-start.1
  6.9 0.0 copy-start.3
  6.9 0.0 copy-start.5
  6.9 8.8 %all-to-all-start = ((bf16[32,16,512]{2,1,0:T(8,128)(2,1)}), bf16[32,16,512]{2,1,0:T(8,128)(2,1)S(1)}, u32[]{:S(2)}, u32[]{:S(2)}) async-start(bf16[32,16,512]{2,1,0:T(8,128)(2,1)} %get-tuple-element.28), calls=%async_computation | async-start | bytes 1048576 | tf_op jit(solution)/shard_map/all_to_all | solution.py:372
  15.8 0.0 collective-permute-done.tail_ref
  15.8 0.0 copy-start.4
  15.8 0.0 copy-done.1
  15.8 0.0 copy-done.3
  15.8 0.0 copy-done.5
  15.8 0.6 %copy-done.4 = f32[512]{0:T(512)S(1)} copy-done((f32[512]{0:T(512)S(1)}, f32[512]{0:T(512)}, u32[]{:S(2)}) %copy-start.4) | copy-done | bytes 2072
  16.5 7.0 %direct.1 = (bf16[192,512]{1,0:T(8,128)(2,1)S(1)}, f32[128,512]{1,0:T(8,128)S(1)}, f32[3,16,512]{2,1,0:T(8,128)S(1)}, f32[192,512]{1,0:T(8,128)S(1)}, f32[2,16,512]{2,1,0:T(8,128)S(1)}, /*index=5*/f32[1,512]{1,0:T(1,128)S(1)}) custom-call(s32[1]{0:T(128)} %bitcast.index_ref, bf16[128,512]{1,0:T(8,128)(2,1)S(1)} %copy-done.1, f32[16,512]{1,0:T(8,128)S(1)} %copy-done.2, ...), custom_call_target="tpu_custom_call" | custom-call | flops 8000000000 | tf_op jit(solution)/shard_map/direct/pallas_call | solution.py:323
  23.5 4.0 %all-to-all-done.states_ref = bf16[32,16,512]{2,1,0:T(8,128)(2,1)S(1)} async-done(((bf16[32,16,512]{2,1,0:T(8,128)(2,1)}), bf16[32,16,512]{2,1,0:T(8,128)(2,1)S(1)}, u32[]{:S(2)}, u32[]{:S(2)}) %all-to-all-start) | async-done | bytes 524320 | tf_op jit(solution)/shard_map/all_to_all | solution.py:372
  27.5 0.7 %combine.1 = (f32[192,512]{1,0:T(8,128)S(1)}, f32[8,1,192]{2,1,0:T(1,128)S(1)}) custom-call(s32[1]{0:T(128)} %bitcast.index_ref, f32[128,512]{1,0:T(8,128)S(1)} %get-tuple-element.26.base_ref, f32[3,16,512]{2,1,0:T(8,128)S(1)} %get-tuple-element.27.spans_ref, bf16[32,16,512]{2,1,0:T(8,128)(2,1)S(1)} %all-to-all-done.states_ref, ...), custom_call_target="tpu_custom_call" | custom-call | tf_op jit(solution)/shard_map/combine/pallas_call | solution.py:323
  28.2 13.0 %all_to_all.10 = f32[8,1,192]{2,1,0:T(1,128)S(1)} all-to-all(f32[8,1,192]{2,1,0:T(1,128)S(1)} %get-tuple-element.34), channel_id=1, replica_groups=mesh['ctx'=32,'ch'=8] {'ch'}, dimensions={0} | all-to-all | bytes 12288 | tf_op jit(solution)/shard_map/all_to_all | solution.py:403
  41.2 0.8 %multiply_convert_fusion = bf16[192,512]{1,0:T(8,128)(2,1)} fusion(f32[192,512]{1,0:T(8,128)S(1)} %get-tuple-element.33, f32[192]{0:T(256)S(1)} %add_rsqrt_fusion), kind=kLoop, calls=%fused_computation | loop fusion | flops 196608 | bytes 590592 | tf_op jit(solution)/shard_map/convert_element_type | solution.py:405
  (4 shorter events, 0.1 us)
Async XLA Ops:
  0.0 1.1 %copy-start = (bf16[3,192,512]{2,1,0:T(8,128)(2,1)S(1)}, bf16[3,192,512]{2,1,0:T(8,128)(2,1)}, u32[]{:S(2)}) copy-start(bf16[3,192,512]{2,1,0:T(8,128)(2,1)} %proj_ref.1) | copy-start | bytes 1769476
  1.1 2.8 %copy-start.6 = (f32[7,3,512]{2,0,1:T(8,128)S(1)}, f32[7,3,512]{2,0,1:T(8,128)}, u32[]{:S(2)}) copy-start(f32[7,3,512]{2,0,1:T(8,128)} %param.8) | copy-start | bytes 129028
  1.1 4.8 %collective-permute-start.1 = (bf16[2,16,512]{2,1,0:T(8,128)(2,1)S(1)}, bf16[2,16,512]{2,1,0:T(8,128)(2,1)S(1)}, u32[]{:S(2)}, u32[]{:S(2)}) collective-permute-start(bf16[2,16,512]{2,1,0:T(8,128)(2,1)S(1)} %get-tuple-element.23), channel_id=1, source_target_pairs={{0,8},{8,16},{16,24},{24,32},{32,40},{40,48},{48,56},{56,64},{64,7... | collective-permute-start | bytes 98312 | tf_op jit(solution)/shard_map/ppermute | solution.py:341
  3.9 1.3 %copy-start.2 = (f32[16,512]{1,0:T(8,128)S(1)}, f32[16,512]{1,0:T(8,128)}, u32[]{:S(2)}) copy-start(f32[16,512]{1,0:T(8,128)} %decay_ref.5) | copy-start | bytes 98308
  4.5 11.3 %collective-permute-start = (bf16[144,512]{1,0:T(8,128)(2,1)S(1)}, bf16[144,512]{1,0:T(8,128)(2,1)S(1)}, u32[]{:S(2)}, u32[]{:S(2)}) collective-permute-start(bf16[144,512]{1,0:T(8,128)(2,1)S(1)} %get-tuple-element.21), channel_id=1, source_target_pairs={{0,8},{8,16},{16,24},{24,32},{32,40},{40,48},{48,56},{56,64},{64,7... | collective-permute-start | bytes 442376 | tf_op jit(solution)/shard_map/ppermute | solution.py:341
  6.9 8.9 %copy-start.1 = (bf16[128,512]{1,0:T(8,128)(2,1)S(1)}, bf16[128,512]{1,0:T(8,128)(2,1)}, u32[]{:S(2)}) copy-start(bf16[128,512]{1,0:T(8,128)(2,1)} %med_ref.1) | copy-start | bytes 393220
  6.9 8.9 %copy-start.3 = (f32[16,512]{1,0:T(8,128)S(1)}, f32[16,512]{1,0:T(8,128)}, u32[]{:S(2)}) copy-start(f32[16,512]{1,0:T(8,128)} %res_ref.1) | copy-start | bytes 98308
  6.9 8.9 %copy-start.5 = (f32[512]{0:T(512)S(1)}, f32[512]{0:T(512)}, u32[]{:S(2)}) copy-start(f32[512]{0:T(512)} %param.13) | copy-start | bytes 6148
  6.9 20.6 %all-to-all-start = ((bf16[32,16,512]{2,1,0:T(8,128)(2,1)}), bf16[32,16,512]{2,1,0:T(8,128)(2,1)S(1)}, u32[]{:S(2)}, u32[]{:S(2)}) async-start(bf16[32,16,512]{2,1,0:T(8,128)(2,1)} %get-tuple-element.28), calls=%async_computation | async-start | bytes 1048576 | tf_op jit(solution)/shard_map/all_to_all | solution.py:372
  15.8 0.7 %copy-start.4 = (f32[512]{0:T(512)S(1)}, f32[512]{0:T(512)}, u32[]{:S(2)}) copy-start(f32[512]{0:T(512)} %param.12) | copy-start | bytes 6148

commit v8 on v7

--- a/solution.py
+++ b/solution.py
@@ -46,12 +46,6 @@
             state = state * step + tile
         sums.append(jnp.sum(state * jnp.exp(-decay[n : n + 1] * (TILE - 1 - rows)), axis=0, keepdims=True))
     return jnp.concatenate(sums, 0)
-
-
-def edge_kernel(proj_ref, edge_ref, raw_ref):
-    rows = proj_ref.shape[1]
-    edge_ref[...] = proj_ref[1:, rows - EDGE :]
-    raw_ref[...] = proj_ref[...]
 
 
 def short_sum(ext, taps, start, rows, first=0):
@@ -346,9 +340,8 @@
     ctx, ch = lax.axis_size("ctx"), lax.axis_size("ch")
     index = lax.axis_index("ctx").reshape(1)
     short = jnp.pad(jnp.transpose(short_filter, (1, 0, 2)), ((0, 0), (0, TILE - SHORT), (0, 0)))
-    edge, raw = call(
-        edge_kernel, "edge", (shape((2, EDGE, chans), BF16), shape(projected.shape, BF16)), [], (projected,)
-    )
+    raw = projected
+    edge = projected[1:, rows - EDGE :]
     halo = from_behind(edge, "ctx")
     product, tail, head = call(
         feature_kernel,

time: 42.4 us -> 42.5 us (level)
  starting transfers between devices: 12.3 us -> 11.2 us
  local copies, waits for them, and re-layouts: 1.74 us -> 2.57 us
  blocking collectives: 13 us -> 13.5 us
    slice x0 -> x1, local copies, waits for them, and re-layouts: none -> 0.77 us  [on_device(): edge = projected[1:, rows - EDGE:]]
    ppermute x2, starting transfers between devices: 3.51 us -> 2.8 us  [from_behind(): return lax.ppermute(block, axis, [(i, (i + 1) % size) for i in range(size)])]
    all_to_all x1, blocking collectives: 13 us -> 13.5 us  [on_device(): sums = lax.all_to_all(sums, 'ch', 0, 0, tiled=True)]
    all_to_all x1, starting transfers between devices: 8.84 us -> 8.35 us  [on_device(): states = lax.all_to_all(spread, 'ctx', 0, 0, tiled=True)]
    unnamed x14 -> x16, local copies, waits for them, and re-layouts: 1.73 us -> 1.79 us
    pallas_call x6 -> x5, Pallas kernels: 10.1 us -> 10 us  [call(): pl.pallas_call(kernel, out_shape=out_shape, in_specs=[smem] * scalars + [...]
where the time goes in v8:
time: 42.5 us; the launch traced here: 42.1 us
  blocking collectives  13.5 us (32%)
  starting transfers between devices  11.2 us (26%)
  Pallas kernels  10 us (24%)
  waiting for transfers between devices  4.01 us (9%)
  local copies, waits for them, and re-layouts  2.57 us (6%)
  other arithmetic  0.81 us (2%)
    all_to_all x1, blocking collectives, on_device(): sums = lax.all_to_all(sums, 'ch', 0, 0, tiled=True)  13.5 us
    pallas_call x5, Pallas kernels, call(): pl.pallas_call(kernel, out_shape=out_shape, in_specs=[smem] * scalars + [...  10 us
    all_to_all x1, starting transfers between devices, on_device(): states = lax.all_to_all(spread, 'ctx', 0, 0, tiled=True)  8.35 us
    all_to_all x1, waiting for transfers between devices, on_device(): states = lax.all_to_all(spread, 'ctx', 0, 0, tiled=True)  4.01 us
    ppermute x2, starting transfers between devices, from_behind(): return lax.ppermute(block, axis, [(i, (i + 1) % size) for i in range(size)])  2.8 us
    unnamed x16, local copies, waits for them, and re-layouts  1.79 us
  transfers between devices with their start and end apart: 3, of which 1 were waited for; matrix products, arithmetic and copies ran while one was open for 0% of the time, Pallas kernels for 22%

profile of v8, /device:TPU:1, one launch (start us, length us, event | category | flops | bytes accessed | tf_op | source)
XLA Modules:
  0.0 42.1 jit_solution(824259882899882851)
XLA Ops:
  0.0 0.0 copy-start.7
  0.0 0.8 %slice.3 = bf16[2,16,512]{2,1,0:T(8,128)(2,1)S(1)} slice(bf16[3,192,512]{2,1,0:T(8,128)(2,1)} %raw_ref.3), slice={[1:3], [176:192], [0:512]} | slice | bytes 65536 | tf_op jit(solution)/shard_map/slice | solution.py:344
  0.8 2.7 %collective-permute-start.1 = (bf16[2,16,512]{2,1,0:T(8,128)(2,1)S(1)}, bf16[2,16,512]{2,1,0:T(8,128)(2,1)S(1)}, u32[]{:S(2)}, u32[]{:S(2)}) collective-permute-start(bf16[2,16,512]{2,1,0:T(8,128)(2,1)S(1)} %slice.3), channel_id=1, source_target_pairs={{0,8},{8,16},{16,24},{24,32},{32,40},{40,48},{48,56},{56,64},{64,7... | collective-permute-start | bytes 98312 | tf_op jit(solution)/shard_map/ppermute | solution.py:335
  3.5 0.0 copy-done.7
  3.5 0.0 copy-start
  3.5 1.1 %copy-done = bf16[3,192,512]{2,1,0:T(8,128)(2,1)S(1)} copy-done((bf16[3,192,512]{2,1,0:T(8,128)(2,1)S(1)}, bf16[3,192,512]{2,1,0:T(8,128)(2,1)}, u32[]{:S(2)}) %copy-start) | copy-done | bytes 589848
  4.5 0.0 copy-start.3
  4.5 0.6 %features.1 = (bf16[192,512]{1,0:T(8,128)(2,1)S(1)}, bf16[144,512]{1,0:T(8,128)(2,1)S(1)}, f32[2,8,512]{2,1,0:T(8,128)S(1)}) custom-call(bf16[3,192,512]{2,1,0:T(8,128)(2,1)S(1)} %copy-done, f32[3,8,512]{2,1,0:T(8,128)S(1)} %pad.4.short_ref), custom_call_target="tpu_custom_call" | custom-call | flops 2000000000 | tf_op jit(solution)/shard_map/features/pallas_call | solution.py:317
  5.1 0.1 collective-permute-start
  5.2 0.1 copy-done.3
  5.3 0.7 %states.1.sums_ref = f32[2,16,512]{2,1,0:T(8,128)S(1)} custom-call(bf16[192,512]{1,0:T(8,128)(2,1)S(1)} %get-tuple-element.19.p_ref, f32[16,512]{1,0:T(8,128)S(1)} %copy-done.3), custom_call_target="tpu_custom_call" | custom-call | flops 1000000000 | tf_op jit(solution)/shard_map/states/pallas_call | solution.py:317
  6.0 0.0 collective-permute-done.1.halo_ref
  6.0 1.0 %first.1 = (bf16[32,16,512]{2,1,0:T(8,128)(2,1)}, f32[8,512]{1,0:T(8,128)S(1)}) custom-call(s32[1]{0:T(128)} %bitcast.index_ref, bf16[2,16,512]{2,1,0:T(8,128)(2,1)S(1)} %collective-permute-done.1.halo_ref, f32[2,8,512]{2,1,0:T(8,128)S(1)} %get-tuple-element.20.head_ref, f32[3,8,512]{2,1,0:T(8,128)S(1)} %pad.4.short_ref, f32[16,512]{1,0:T(8,128)S(1)} %copy-done.3, ...), custom_call_target="tpu_custom_call" | custom-call | flops 2000000000 | tf_op jit(solution)/shard_map/first/pallas_call | solution.py:317
  7.0 0.0 copy-start.1
  7.0 0.0 copy-start.2
  7.0 0.0 copy-start.4
  7.0 0.0 copy-start.6
  7.0 8.4 %all-to-all-start = ((bf16[32,16,512]{2,1,0:T(8,128)(2,1)}), bf16[32,16,512]{2,1,0:T(8,128)(2,1)S(1)}, u32[]{:S(2)}, u32[]{:S(2)}) async-start(bf16[32,16,512]{2,1,0:T(8,128)(2,1)} %get-tuple-element.24), calls=%async_computation | async-start | bytes 1048576 | tf_op jit(solution)/shard_map/all_to_all | solution.py:365
  15.4 0.0 collective-permute-done.tail_ref
  15.4 0.0 copy-start.5
  15.4 0.0 copy-done.1
  15.4 0.0 copy-done.2
  15.4 0.0 copy-done.4
  15.4 0.0 copy-done.6
  15.4 0.6 %copy-done.5 = f32[512]{0:T(512)S(1)} copy-done((f32[512]{0:T(512)S(1)}, f32[512]{0:T(512)}, u32[]{:S(2)}) %copy-start.5) | copy-done | bytes 2072
  16.1 7.0 %direct.1 = (bf16[192,512]{1,0:T(8,128)(2,1)S(1)}, f32[128,512]{1,0:T(8,128)S(1)}, f32[3,16,512]{2,1,0:T(8,128)S(1)}, f32[192,512]{1,0:T(8,128)S(1)}, f32[2,16,512]{2,1,0:T(8,128)S(1)}, /*index=5*/f32[1,512]{1,0:T(1,128)S(1)}) custom-call(s32[1]{0:T(128)} %bitcast.index_ref, bf16[128,512]{1,0:T(8,128)(2,1)S(1)} %copy-done.2, f32[16,512]{1,0:T(8,128)S(1)} %copy-done.3, ...), custom_call_target="tpu_custom_call" | custom-call | flops 8000000000 | tf_op jit(solution)/shard_map/direct/pallas_call | solution.py:317
  23.1 4.0 %all-to-all-done.states_ref = bf16[32,16,512]{2,1,0:T(8,128)(2,1)S(1)} async-done(((bf16[32,16,512]{2,1,0:T(8,128)(2,1)}), bf16[32,16,512]{2,1,0:T(8,128)(2,1)S(1)}, u32[]{:S(2)}, u32[]{:S(2)}) %all-to-all-start) | async-done | bytes 524320 | tf_op jit(solution)/shard_map/all_to_all | solution.py:365
  27.1 0.7 %combine.1 = (f32[192,512]{1,0:T(8,128)S(1)}, f32[8,1,192]{2,1,0:T(1,128)S(1)}) custom-call(s32[1]{0:T(128)} %bitcast.index_ref, f32[128,512]{1,0:T(8,128)S(1)} %get-tuple-element.22.base_ref, f32[3,16,512]{2,1,0:T(8,128)S(1)} %get-tuple-element.23.spans_ref, bf16[32,16,512]{2,1,0:T(8,128)(2,1)S(1)} %all-to-all-done.states_ref, ...), custom_call_target="tpu_custom_call" | custom-call | tf_op jit(solution)/shard_map/combine/pallas_call | solution.py:317
  27.8 13.5 %all_to_all.10 = f32[8,1,192]{2,1,0:T(1,128)S(1)} all-to-all(f32[8,1,192]{2,1,0:T(1,128)S(1)} %get-tuple-element.30), channel_id=1, replica_groups=mesh['ctx'=32,'ch'=8] {'ch'}, dimensions={0} | all-to-all | bytes 12288 | tf_op jit(solution)/shard_map/all_to_all | solution.py:396
  41.3 0.8 %multiply_convert_fusion = bf16[192,512]{1,0:T(8,128)(2,1)} fusion(f32[192,512]{1,0:T(8,128)S(1)} %get-tuple-element.29, f32[192]{0:T(256)S(1)} %add_rsqrt_fusion), kind=kLoop, calls=%fused_computation | loop fusion | flops 196608 | bytes 590592 | tf_op jit(solution)/shard_map/convert_element_type | solution.py:398
  (3 shorter events, 0.0 us)
Async XLA Ops:
  0.0 3.5 %copy-start.7 = (f32[7,3,512]{2,0,1:T(8,128)S(1)}, f32[7,3,512]{2,0,1:T(8,128)}, u32[]{:S(2)}) copy-start(f32[7,3,512]{2,0,1:T(8,128)} %param.8) | copy-start | bytes 129028
  0.8 5.2 %collective-permute-start.1 = (bf16[2,16,512]{2,1,0:T(8,128)(2,1)S(1)}, bf16[2,16,512]{2,1,0:T(8,128)(2,1)S(1)}, u32[]{:S(2)}, u32[]{:S(2)}) collective-permute-start(bf16[2,16,512]{2,1,0:T(8,128)(2,1)S(1)} %slice.3), channel_id=1, source_target_pairs={{0,8},{8,16},{16,24},{24,32},{32,40},{40,48},{48,56},{56,64},{64,7... | collective-permute-start | bytes 98312 | tf_op jit(solution)/shard_map/ppermute | solution.py:335
  3.5 1.1 %copy-start = (bf16[3,192,512]{2,1,0:T(8,128)(2,1)S(1)}, bf16[3,192,512]{2,1,0:T(8,128)(2,1)}, u32[]{:S(2)}) copy-start(bf16[3,192,512]{2,1,0:T(8,128)(2,1)} %raw_ref.3) | copy-start | bytes 1769476
  4.5 0.8 %copy-start.3 = (f32[16,512]{1,0:T(8,128)S(1)}, f32[16,512]{1,0:T(8,128)}, u32[]{:S(2)}) copy-start(f32[16,512]{1,0:T(8,128)} %decay_ref.5) | copy-start | bytes 98308
  5.1 10.3 %collective-permute-start = (bf16[144,512]{1,0:T(8,128)(2,1)S(1)}, bf16[144,512]{1,0:T(8,128)(2,1)S(1)}, u32[]{:S(2)}, u32[]{:S(2)}) collective-permute-start(bf16[144,512]{1,0:T(8,128)(2,1)S(1)} %get-tuple-element.18), channel_id=1, source_target_pairs={{0,8},{8,16},{16,24},{24,32},{32,40},{40,48},{48,56},{56,64},{64,7... | collective-permute-start | bytes 442376 | tf_op jit(solution)/shard_map/ppermute | solution.py:335
  7.0 8.4 %copy-start.1 = (bf16[3,192,512]{2,1,0:T(8,128)(2,1)S(1)}, bf16[3,192,512]{2,1,0:T(8,128)(2,1)}, u32[]{:S(2)}) copy-start(bf16[3,192,512]{2,1,0:T(8,128)(2,1)} %raw_ref.3) | copy-start | bytes 1769476
  7.0 8.4 %copy-start.2 = (bf16[128,512]{1,0:T(8,128)(2,1)S(1)}, bf16[128,512]{1,0:T(8,128)(2,1)}, u32[]{:S(2)}) copy-start(bf16[128,512]{1,0:T(8,128)(2,1)} %med_ref.1) | copy-start | bytes 393220
  7.0 8.4 %copy-start.4 = (f32[16,512]{1,0:T(8,128)S(1)}, f32[16,512]{1,0:T(8,128)}, u32[]{:S(2)}) copy-start(f32[16,512]{1,0:T(8,128)} %res_ref.1) | copy-start | bytes 98308
  7.0 8.4 %copy-start.6 = (f32[512]{0:T(512)S(1)}, f32[512]{0:T(512)}, u32[]{:S(2)}) copy-start(f32[512]{0:T(512)} %param.13) | copy-start | bytes 6148
  7.0 20.1 %all-to-all-start = ((bf16[32,16,512]{2,1,0:T(8,128)(2,1)}), bf16[32,16,512]{2,1,0:T(8,128)(2,1)S(1)}, u32[]{:S(2)}, u32[]{:S(2)}) async-start(bf16[32,16,512]{2,1,0:T(8,128)(2,1)} %get-tuple-element.24), calls=%async_computation | async-start | bytes 1048576 | tf_op jit(solution)/shard_map/all_to_all | solution.py:365
  15.4 0.7 %copy-start.5 = (f32[512]{0:T(512)S(1)}, f32[512]{0:T(512)}, u32[]{:S(2)}) copy-start(f32[512]{0:T(512)} %param.12) | copy-start | bytes 6148
